TPU v7x, 32 devices: a whole 2x2x4 slice. The times are simulated.
32 devices in a mesh: ctx: 8 (over z, y), fsdp: 4 (over x, core).
Axes of the slice: x: 2, y: 2, z: 4, core: 2. Of those that a mesh axis runs over, the one named last changes fastest.
Arguments:
- inputs: bfloat16 [2, 2048, 1024], P(None, ('ctx', 'fsdp')), may hold values from -6 to 6
- attn_gain: bfloat16 [1024], P('fsdp'), may hold values from 0.5 to 1.5
- attn_proj: bfloat16 [1024, 3072], P('fsdp'), may hold values from -0.1875 to 0.1875
- attn_out: bfloat16 [1024, 1024], P('fsdp'), may hold values from -6 to 6
- mlp_gain: bfloat16 [1024], P('fsdp'), may hold values from 0.5 to 1.5
- mlp_in: bfloat16 [1024, 5248], P('fsdp'), may hold values from -0.1875 to 0.1875
- mlp_out: bfloat16 [2624, 1024], P('fsdp'), may hold values from -0.125 to 0.125
- cotangent: bfloat16 [2, 2048, 1024], P(None, ('ctx', 'fsdp')), may hold values from -6 to 6
Outputs:
- outputs: bfloat16 [2, 2048, 1024], P(None, ('ctx', 'fsdp'))
- input_grad: float32 [2, 2048, 1024], P(None, ('ctx', 'fsdp'))
- attn_gain_grad: float32 [1024], P('fsdp')
- attn_proj_grad: float32 [1024, 3072], P('fsdp')
- attn_out_grad: float32 [1024, 1024], P('fsdp')
- mlp_gain_grad: float32 [1024], P('fsdp')
- mlp_in_grad: float32 [1024, 5248], P('fsdp')
- mlp_out_grad: float32 [2624, 1024], P('fsdp')
All inputs are finite; a program needn't handle non-finite values.
Results may differ from a plain program's by a relative error of at most 0.02.
Values may be sent and summed in bfloat16 or wider, within the bound.
A program may use at most 768 MiB of HBM per device.

v0:
```python
import jax
import jax.numpy as jnp
from jax import lax
from jax.sharding import PartitionSpec as P

HEADS = 16
HEAD_DIM = 64


eps = 1e-05
rope_base = 160000.0


def layer_norm(values, norm_gain):
    center = jnp.mean(values, axis=-1, keepdims=True)
    centred = values - center
    spread = jnp.mean(centred * centred, axis=-1, keepdims=True)
    return centred * lax.rsqrt(spread + eps) * norm_gain


def rotate(values, cos_table, sin_table):
    halfway = values.shape[-1] // 2
    turned = jnp.concatenate([-values[..., halfway:], values[..., :halfway]], axis=-1)
    return values * cos_table + turned * sin_table


def unrotate(gradient, cos_table, sin_table):
    halfway = gradient.shape[-1] // 2
    sined = gradient * sin_table
    return gradient * cos_table + jnp.concatenate(
        [sined[..., halfway:], -sined[..., :halfway]], axis=-1
    )


def angles(positions, head_size):
    exponent = jnp.arange(0, head_size, 2, dtype=jnp.float32) / head_size
    inverse = rope_base ** (-exponent)
    phases = positions.astype(jnp.float32)[:, None] * inverse[None, :]
    phases = jnp.concatenate([phases, phases], axis=-1)
    return (jnp.cos(phases)[:, None, :], jnp.sin(phases)[:, None, :])


def gated_unit(lifted):
    hidden_units = lifted.shape[-1] // 2
    return jax.nn.gelu(lifted[..., :hidden_units], approximate=False) * lifted[..., hidden_units:]


def as_heads(flat_rows, head_size):
    return flat_rows.reshape(flat_rows.shape[0], flat_rows.shape[1], -1, head_size)


def empty_state(seq_count, head_count, query_rows, head_size):
    return (
        jnp.full((seq_count, head_count, query_rows), -jnp.inf, jnp.float32),
        jnp.zeros((seq_count, head_count, query_rows), jnp.float32),
        jnp.zeros((seq_count, head_count, query_rows, head_size), jnp.float32),
    )


def forward_step(queries, scaling, state_now, shard_part):
    running_max, denominator, weighted = state_now
    key_part = as_heads(shard_part[0], queries.shape[3])
    value_part = as_heads(shard_part[1], queries.shape[3])
    scores = (
        jnp.einsum("sqhd,skhd->shqk", queries, key_part, preferred_element_type=jnp.float32)
        * scaling
    )
    new_max = jnp.max(scores, axis=-1)
    fading = jnp.exp(running_max - new_max)
    weights = jnp.exp(scores - new_max[..., None])
    denominator = denominator * fading + jnp.sum(weights, axis=-1)
    weighted = weighted * fading[..., None] + jnp.einsum(
        "shqk,skhd->shqd",
        weights.astype(jnp.bfloat16),
        value_part,
        preferred_element_type=jnp.float32,
    )
    return (new_max, denominator, weighted)


def query_step(queries, grad_out, log_total, inner_heads, scaling, shard_part):
    key_part = as_heads(shard_part[0], queries.shape[3])
    value_part = as_heads(shard_part[1], queries.shape[3])
    scores = (
        jnp.einsum("sqhd,skhd->shqk", queries, key_part, preferred_element_type=jnp.float32)
        * scaling
    )
    weights = jnp.exp(scores - log_total[..., None])
    weight_grad = jnp.einsum(
        "sqhd,skhd->shqk", grad_out, value_part, preferred_element_type=jnp.float32
    )
    score_grad = (weights * (weight_grad - inner_heads[..., None])).astype(jnp.bfloat16)
    return jnp.einsum("shqk,skhd->sqhd", score_grad, key_part, preferred_element_type=jnp.float32)


def key_step(key_heads, value_heads, scaling, shard_part):
    head_size = key_heads.shape[3]
    query_part = as_heads(shard_part[0].astype(jnp.bfloat16), head_size)
    grad_part = as_heads(shard_part[1].astype(jnp.bfloat16), head_size)
    log_part = shard_part[2].transpose(0, 2, 1)
    inner_part = shard_part[3].transpose(0, 2, 1)
    scores = (
        jnp.einsum("sqhd,skhd->shqk", query_part, key_heads, preferred_element_type=jnp.float32)
        * scaling
    )
    weights = jnp.exp(scores - log_part[..., None])
    value_grad = jnp.einsum(
        "shqk,sqhd->skhd",
        weights.astype(jnp.bfloat16),
        grad_part,
        preferred_element_type=jnp.float32,
    )
    weight_grad = jnp.einsum(
        "sqhd,skhd->shqk", grad_part, value_heads, preferred_element_type=jnp.float32
    )
    score_grad = (weights * (weight_grad - inner_part[..., None])).astype(jnp.bfloat16)
    key_grad = jnp.einsum(
        "shqk,sqhd->skhd", score_grad, query_part, preferred_element_type=jnp.float32
    )
    return (key_grad, value_grad)


def on_device(inputs, attn_gain, attn_proj, attn_out, mlp_gain, mlp_in, mlp_out, cotangent):
    seq_count, row_count, model_width = inputs.shape
    head_size = HEAD_DIM
    head_count = HEADS
    scaling = head_size ** (-0.5)
    fsdp_count = lax.axis_size("fsdp")
    fsdp_place = lax.axis_index("fsdp")
    start_row = (lax.axis_index("ctx") * fsdp_count + fsdp_place) * row_count
    cos_table, sin_table = angles(start_row + jnp.arange(row_count, dtype=jnp.int32), head_size)
    tokens = seq_count * row_count
    gain_one, proj_full, out_full = (
        lax.all_gather(attn_gain, "fsdp", axis=0, tiled=True),
        lax.all_gather(attn_proj, "fsdp", axis=0, tiled=True),
        lax.all_gather(attn_out, "fsdp", axis=0, tiled=True),
    )
    states = inputs.astype(jnp.float32)
    normed, norm_back_one = jax.vjp(layer_norm, states, gain_one.astype(jnp.float32))
    normed_low = normed.astype(jnp.bfloat16).reshape(tokens, model_width)
    mixed_rows = jnp.dot(normed_low, proj_full, preferred_element_type=jnp.float32).reshape(
        seq_count, row_count, 3, head_count, head_size
    )
    queries = rotate(mixed_rows[:, :, 0], cos_table, sin_table).astype(jnp.bfloat16)
    key_flat = (
        rotate(mixed_rows[:, :, 1], cos_table, sin_table)
        .astype(jnp.bfloat16)
        .reshape(seq_count, row_count, model_width)
    )
    value_flat = mixed_rows[:, :, 2].astype(jnp.bfloat16).reshape(seq_count, row_count, model_width)
    key_block, value_block = (
        lax.all_gather(key_flat, "fsdp", axis=1, tiled=True),
        lax.all_gather(value_flat, "fsdp", axis=1, tiled=True),
    )
    start_state = empty_state(seq_count, head_count, row_count, head_size)
    running_max, denominator, weighted = forward_step(
        queries,
        scaling,
        start_state,
        (
            lax.all_gather(key_block, "ctx", axis=1, tiled=True),
            lax.all_gather(value_block, "ctx", axis=1, tiled=True),
        ),
    )
    context = (weighted / denominator[..., None]).transpose(0, 2, 1, 3)
    log_total = running_max + jnp.log(denominator)
    context_low = context.reshape(tokens, model_width).astype(jnp.bfloat16)
    branch = jnp.dot(context_low, out_full, preferred_element_type=jnp.float32).reshape(
        seq_count, row_count, model_width
    )
    middle = states + branch
    gain_two, lift_full, down_full = (
        lax.all_gather(mlp_gain, "fsdp", axis=0, tiled=True),
        lax.all_gather(mlp_in, "fsdp", axis=0, tiled=True),
        lax.all_gather(mlp_out, "fsdp", axis=0, tiled=True),
    )
    normed_two, norm_back_two = jax.vjp(layer_norm, middle, gain_two.astype(jnp.float32))
    normed_two_low = normed_two.astype(jnp.bfloat16).reshape(tokens, model_width)
    lifted = jnp.dot(normed_two_low, lift_full, preferred_element_type=jnp.float32)
    gate_out, gated_back = jax.vjp(gated_unit, lifted)
    gate_low = gate_out.astype(jnp.bfloat16)
    outputs = (
        middle
        + jnp.dot(gate_low, down_full, preferred_element_type=jnp.float32).reshape(
            seq_count, row_count, model_width
        )
    ).astype(jnp.bfloat16)
    seed_rows = cotangent.reshape(tokens, model_width)
    gate_grad = jnp.einsum("td,fd->tf", seed_rows, down_full, preferred_element_type=jnp.float32)
    lifted_grad = gated_back(gate_grad)[0].astype(jnp.bfloat16)
    normed_two_grad = jnp.einsum(
        "tf,wf->tw", lifted_grad, lift_full, preferred_element_type=jnp.float32
    ).reshape(seq_count, row_count, model_width)
    middle_part, gain_two_grad = norm_back_two(normed_two_grad)
    middle_grad = cotangent.astype(jnp.float32) + middle_part
    down_grad = jnp.einsum("tf,td->fd", gate_low, seed_rows, preferred_element_type=jnp.float32)
    lift_grad = jnp.einsum(
        "tw,tf->wf", normed_two_low, lifted_grad, preferred_element_type=jnp.float32
    )
    gain_two_sum, lift_sum, down_sum = (
        lax.psum_scatter(gain_two_grad, "fsdp", scatter_dimension=0, tiled=True),
        lax.psum_scatter(lift_grad, "fsdp", scatter_dimension=0, tiled=True),
        lax.psum_scatter(down_grad, "fsdp", scatter_dimension=0, tiled=True),
    )
    lift_sum, down_sum = lax.psum((lift_sum, down_sum), "ctx")
    middle_low = middle_grad.reshape(tokens, model_width).astype(jnp.bfloat16)
    context_grad = (
        jnp.einsum("tv,wv->tw", middle_low, out_full, preferred_element_type=jnp.float32)
        .astype(jnp.bfloat16)
        .reshape(seq_count, row_count, head_count, head_size)
    )
    inner = jnp.sum(context_grad.astype(jnp.float32) * context, axis=-1)
    inner_heads = inner.transpose(0, 2, 1)
    log_rows = log_total.transpose(0, 2, 1)
    query_grad = query_step(
        queries,
        context_grad,
        log_total,
        inner_heads,
        scaling,
        (
            lax.all_gather(key_block, "ctx", axis=1, tiled=True),
            lax.all_gather(value_block, "ctx", axis=1, tiled=True),
        ),
    )
    block_len = key_block.shape[1]
    query_wide = queries.reshape(seq_count, row_count, model_width).astype(jnp.float32)
    grad_wide = context_grad.reshape(seq_count, row_count, model_width).astype(jnp.float32)
    key_grad, value_grad = key_step(
        as_heads(key_block, head_size),
        as_heads(value_block, head_size),
        scaling,
        (
            lax.all_gather(query_wide, "ctx", axis=1, tiled=True),
            lax.all_gather(grad_wide, "ctx", axis=1, tiled=True),
            lax.all_gather(log_rows, "ctx", axis=1, tiled=True),
            lax.all_gather(inner, "ctx", axis=1, tiled=True),
        ),
    )
    key_own, value_own = (
        lax.psum_scatter(
            key_grad.reshape(seq_count, block_len, model_width),
            "fsdp",
            scatter_dimension=1,
            tiled=True,
        ),
        lax.psum_scatter(
            value_grad.reshape(seq_count, block_len, model_width),
            "fsdp",
            scatter_dimension=1,
            tiled=True,
        ),
    )
    query_pre = unrotate(query_grad * scaling, cos_table, sin_table)
    key_pre = unrotate(
        key_own.reshape(seq_count, row_count, head_count, head_size) * scaling, cos_table, sin_table
    )
    value_pre = value_own.reshape(seq_count, row_count, head_count, head_size)
    mixed_grad = (
        jnp.stack([query_pre, key_pre, value_pre], axis=2)
        .reshape(tokens, 3 * model_width)
        .astype(jnp.bfloat16)
    )
    normed_grad = jnp.einsum(
        "tm,wm->tw", mixed_grad, proj_full, preferred_element_type=jnp.float32
    ).reshape(seq_count, row_count, model_width)
    state_part, gain_one_grad = norm_back_one(normed_grad)
    input_grad = middle_grad + state_part
    out_grad = jnp.einsum("tw,tv->wv", context_low, middle_low, preferred_element_type=jnp.float32)
    proj_grad = jnp.einsum("tw,tm->wm", normed_low, mixed_grad, preferred_element_type=jnp.float32)
    gain_one_sum, proj_sum, out_sum = (
        lax.psum_scatter(gain_one_grad, "fsdp", scatter_dimension=0, tiled=True),
        lax.psum_scatter(proj_grad, "fsdp", scatter_dimension=0, tiled=True),
        lax.psum_scatter(out_grad, "fsdp", scatter_dimension=0, tiled=True),
    )
    gain_one_sum, gain_two_sum, proj_sum, out_sum = lax.psum(
        (gain_one_sum, gain_two_sum, proj_sum, out_sum), "ctx"
    )
    return (outputs, input_grad, gain_one_sum, proj_sum, out_sum, gain_two_sum, lift_sum, down_sum)


def solution(mesh):
    in_specs = (
        P(None, ("ctx", "fsdp"), None),
        P("fsdp"),
        P("fsdp", None),
        P("fsdp", None),
        P("fsdp"),
        P("fsdp", None),
        P("fsdp", None),
        P(None, ("ctx", "fsdp"), None),
    )
    out_specs = (
        P(None, ("ctx", "fsdp"), None),
        P(None, ("ctx", "fsdp"), None),
        P("fsdp"),
        P("fsdp", None),
        P("fsdp", None),
        P("fsdp"),
        P("fsdp", None),
        P("fsdp", None),
    )
    return jax.shard_map(
        on_device, mesh=mesh, in_specs=in_specs, out_specs=out_specs, check_vma=False
    )
```

profile of v0, /device:TPU:0, one launch (start us, length us, event | category | flops | bytes accessed | tf_op | source)
XLA Modules:
  0.0 1542.2 jit_solution(2992624092108072681)
XLA Ops:
  8.6 6.0 all-gather
  16.7 42.0 %all-gather.13.cloned.1.call-done = bf16[1024,3072]{1,0:T(8,128)(2,1)} async-done(((bf16[256,3072]{1,0:T(8,128)(2,1)}), bf16[1024,3072]{1,0:T(8,128)(2,1)}) %all-gather.13.cloned.1.call-update) | async-done | bytes 6291472 | tf_op jit(solution)/shard_map/all_gather | solution.py:135
  58.7 8.7 copy.99
  67.4 4.5 fusion.59
  71.9 2.0 fusion.79
  75.9 2.3 copy.139
  80.6 1.5 copy.137
  82.2 1.5 fusion.58
  84.8 1.3 slice.96
  87.1 14.5 all-gather.15.cloned.1.call-done
  101.7 18.8 %all-gather.19.cloned.1.call-done = bf16[2,256,1024]{2,0,1:T(2,128)(2,1)} async-done(((bf16[2,64,1024]{2,0,1:T(2,128)(2,1)}), bf16[2,256,1024]{2,0,1:T(2,128)(2,1)}) %all-gather.19.cloned.1.call-update) | async-done | bytes 1048592 | tf_op jit(solution)/shard_map/all_gather | solution.py:153
  122.7 5.1 all-gather.1
  128.8 118.6 %all-gather.17.cloned.1.call-done = bf16[2,2048,1024]{2,0,1:T(2,128)(2,1)} async-done(((bf16[2,256,1024]{2,0,1:T(2,128)(2,1)}), bf16[2,2048,1024]{2,0,1:T(2,128)(2,1)}) %all-gather.17.cloned.1.call-update) | async-done | bytes 8388624 | tf_op jit(solution)/shard_map/all_gather | solution.py:161
  247.5 21.3 %copy.105 = bf16[2,2048,1024]{1,2,0:T(8,128)(2,1)} copy(bf16[2,2048,1024]{2,0,1:T(2,128)(2,1)} %all-gather.17.cloned.1.call-done) | data formatting | bytes 16777216 | tf_op jit(solution)/shard_map/all_gather | solution.py:161
  268.8 5.4 multiply_reduce_fusion
  274.2 3.4 fusion
  277.6 2.4 copy-done
  280.0 92.6 %all-gather.21.cloned.1.call-done = bf16[2,2048,1024]{2,0,1:T(2,128)(2,1)} async-done(((bf16[2,256,1024]{2,0,1:T(2,128)(2,1)}), bf16[2,2048,1024]{2,0,1:T(2,128)(2,1)}) %all-gather.21.cloned.1.call-update) | async-done | bytes 8388624 | tf_op jit(solution)/shard_map/all_gather | solution.py:162
  372.6 21.3 %copy.108 = bf16[2,2048,1024]{1,2,0:T(8,128)(2,1)} copy(bf16[2,2048,1024]{2,0,1:T(2,128)(2,1)} %all-gather.21.cloned.1.call-done) | data formatting | bytes 16777216 | tf_op jit(solution)/shard_map/all_gather | solution.py:162
  393.9 11.7 fusion.81
  405.6 2.7 fusion.82
  408.7 59.4 %all-gather.25.cloned.1.call-done = bf16[1024,5248]{1,0:T(8,128)(2,1)} async-done(((bf16[256,5248]{1,0:T(8,128)(2,1)}), bf16[1024,5248]{1,0:T(8,128)(2,1)}) %all-gather.25.cloned.1.call-update) | async-done | bytes 10747920 | tf_op jit(solution)/shard_map/all_gather | solution.py:174
  468.1 7.3 fusion.83
  475.4 35.4 %all-gather.27.cloned.1.call-done = bf16[2624,1024]{1,0:T(8,128)(2,1)} async-done(((bf16[656,1024]{1,0:T(8,128)(2,1)}), bf16[2624,1024]{1,0:T(8,128)(2,1)}) %all-gather.27.cloned.1.call-update) | async-done | bytes 5373968 | tf_op jit(solution)/shard_map/all_gather | solution.py:175
  510.8 8.2 fusion.56
  520.0 5.7 fusion.63
  525.9 3.5 fusion.84
  533.0 1.5 convolution_convert_fusion
  534.6 4.2 copy.118
  538.7 2.2 copy.122
  540.9 21.4 %all-gather.29.cloned.1.call-done = bf16[2,512,1024]{2,0,1:T(2,128)(2,1)} async-done(((bf16[2,64,1024]{2,0,1:T(2,128)(2,1)}), bf16[2,512,1024]{2,0,1:T(2,128)(2,1)}) %all-gather.29.cloned.1.call-update) | async-done | bytes 2097168 | tf_op jit(solution)/shard_map/all_gather | solution.py:234
  562.3 4.7 copy.117
  567.1 10.1 fusion.85
  578.4 32.4 %all_gather.55 = f32[2,512,16]{2,0,1:T(2,128)S(1)} all-gather(f32[2,64,16]{2,0,1:T(2,128)S(1)} %copy.119), channel_id=1, replica_groups=mesh['ctx'=8,'fsdp'=4] {'ctx'}, dimensions={1}, use_global_device_ids=true | all-gather | bytes 73728 | tf_op jit(solution)/shard_map/all_gather | solution.py:236
  611.0 1.5 copy.113
  612.8 31.4 %all_gather.57 = f32[2,512,16]{2,0,1:T(2,128)S(1)} all-gather(f32[2,64,16]{2,0,1:T(2,128)S(1)} %copy.123), channel_id=1, replica_groups=mesh['ctx'=8,'fsdp'=4] {'ctx'}, dimensions={1}, use_global_device_ids=true | all-gather | bytes 73728 | tf_op jit(solution)/shard_map/all_gather | solution.py:237
  644.4 2.9 copy.121
  647.2 11.1 fusion.12
  658.3 4.2 copy.125
  662.5 2.2 copy.132
  664.8 1.4 convert_element_type.147
  666.2 2.7 fusion.87
  670.0 6.5 fusion.88
  678.5 8.6 fusion.3
  687.1 2.9 copy.128
  690.0 57.0 %all-reduce.16 = bf16[2,256,1024]{2,0,1:T(2,128)(2,1)} all-reduce(f32[2,256,1024]{2,0,1:T(2,128)S(1)} %copy.128), channel_id=3, replica_groups=mesh['ctx'=8,'fsdp'=4] {'fsdp'}, use_global_device_ids=true, to_apply=%region_10.0.clone | all-reduce | flops 524288 | bytes 3145728
  750.8 15.6 %broadcast_multiply_fusion.1 = (f32[2,64,16,64]{1,3,2,0:T(8,128)S(1)}, f32[2,64,16,64]{1,3,2,0:T(8,128)}, f32[2,64,16,64]{1,3,2,0:T(8,128)}) fusion(f32[64,64]{0,1:T(8,128)S(1)} %get-tuple-element.45, f32[2,64,16,64]{1,3,2,0:T(8,128)S(1)} %bitcast.140, bf16[2,2048,16,64]{1,3,2,0:T(8,128)(2,1)} %bitcast.134, f32[2,16,64,2048]{3,2,1,0:T(8,128)} %copy-done, ...), kind=kOutput, calls=%fused_computation.82 | convolution fusion | flops 1094975488 | bytes 35946496 | tf_op jit(solution)/shard_map/shqk,skhd->sqhd/dot_general | solution.py:93
  766.4 1.3 slice_bitcast_fusion
  769.2 1.5 maximum_convert_fusion
  770.7 2.5 copy.130
  774.3 6.4 fusion.86
  780.8 14.5 fusion.62
  795.4 70.6 %reduce-scatter.11.cloned.1.call-done = f32[656,1024]{1,0:T(8,128)} async-done(((f32[2624,1024]{1,0:T(8,128)}), f32[656,1024]{1,0:T(8,128)}) %reduce-scatter.11.cloned.1.call-update) | async-done | bytes 2686992 | tf_op jit(solution)/shard_map/reduce_scatter | solution.py:203
  866.1 101.6 %reduce-scatter.5.cloned.1.call-done = f32[256,3072]{1,0:T(8,128)} async-done(((f32[1024,3072]{1,0:T(8,128)}), f32[256,3072]{1,0:T(8,128)}) %reduce-scatter.5.cloned.1.call-update) | async-done | bytes 3145744 | tf_op jit(solution)/shard_map/reduce_scatter | solution.py:273
  967.6 159.0 %reduce-scatter.9.cloned.1.call-done = f32[256,5248]{1,0:T(8,128)} async-done(((f32[1024,5248]{1,0:T(8,128)}), f32[256,5248]{1,0:T(8,128)}) %reduce-scatter.9.cloned.1.call-update) | async-done | bytes 5373968 | tf_op jit(solution)/shard_map/reduce_scatter | solution.py:202
  1127.4 1.3 convert_element_type.145
  1128.8 5.1 fusion.51
  1134.3 5.8 all-reduce.8
  1140.3 23.3 %all-reduce.6 = (f32[256]{0:T(256)}, f32[256]{0:T(256)}) all-reduce(f32[256]{0:T(256)S(1)} %dynamic-slice.5, f32[256]{0:T(256)S(1)} %dynamic-slice.7), channel_id=1, replica_groups=mesh['ctx'=8,'fsdp'=4] {'ctx'}, use_global_device_ids=true, to_apply=%region_15.0 | all-reduce | flops 512 | bytes 4096 | tf_op jit(solution)/shard_map/psum | solution.py:276
  1164.6 359.2 %all-reduce.15.cloned.1.call-done = (f32[256,3072]{1,0:T(8,128)}, f32[256,1024]{1,0:T(8,128)}, f32[256,5248]{1,0:T(8,128)}, f32[656,1024]{1,0:T(8,128)}) async-done(((f32[256,3072]{1,0:T(8,128)}, f32[256,1024]{1,0:T(8,128)}, f32[256,5248]{1,0:T(8,128)}, f32[656,1024]{1,0:T(8,128)}), (f32[256,3072]{1,0:T(8,128)}, f32[256,1024]{1,0:T(8,128)}, f32[256,5248]{1,0:T(8,128)}, ...) | async-done | bytes 12255248 | tf_op jit(solution)/shard_map/psum | solution.py:276
  1523.9 4.0 copy.148
  1527.9 2.3 copy.149
  1530.2 2.7 copy.150
  1533.9 1.5 copy.151
  (171 shorter events, 31.4 us)
Async XLA Ops:
  7.2 8.9 copy-start.1
  7.2 51.5 %all-gather.13.cloned.1.call-start = ((), (), s32[]{:S(2)}) async-start(), calls=%async_computation.4 | async-start | bytes 7864320 | tf_op jit(solution)/shard_map/all_gather | solution.py:135
  7.9 93.7 %all-gather.15.cloned.1.call-start = ((), (), s32[]{:S(2)}) async-start(), calls=%async_computation.5 | async-start | bytes 1310720 | tf_op jit(solution)/shard_map/all_gather | solution.py:152
  14.6 52.8 %copy-start.24 = (f32[4,1,256]{2,1,0:T(1,128)}, f32[4,1,256]{2,1,0:T(1,128)S(1)}, u32[]{:S(2)}) copy-start(f32[4,1,256]{2,1,0:T(1,128)S(1)} %convert_element_type.149) | copy-start | bytes 12292
  16.2 51.2 %copy-start.26 = (f32[2,64]{1,0:T(2,128)}, f32[2,64]{1,0:T(2,128)S(1)}, u32[]{:S(2)}) copy-start(f32[2,64]{1,0:T(2,128)S(1)} %broadcast_multiply_fusion.6) | copy-start | bytes 1540
  16.4 50.9 %copy-start.30 = (f32[2,64]{1,0:T(2,128)}, f32[2,64]{1,0:T(2,128)S(1)}, u32[]{:S(2)}) copy-start(f32[2,64]{1,0:T(2,128)S(1)} %fusion.50) | copy-start | bytes 1540
  16.4 50.9 %copy-start.28 = (f32[2,64]{1,0:T(2,128)}, f32[2,64]{1,0:T(2,128)S(1)}, u32[]{:S(2)}) copy-start(f32[2,64]{1,0:T(2,128)S(1)} %fusion.68) | copy-start | bytes 1540
  16.7 50.7 %copy-start.22 = (bf16[2,64,1024]{2,1,0:T(8,128)(2,1)}, bf16[2,64,1024]{2,1,0:T(8,128)(2,1)S(1)}, u32[]{:S(2)}) copy-start(bf16[2,64,1024]{2,1,0:T(8,128)(2,1)S(1)} %fusion.48) | copy-start | bytes 786436
  71.9 2.3 copy-start.9
  84.7 35.8 %all-gather.19.cloned.1.call-start = ((), (), s32[]{:S(2)}) async-start(), calls=%async_computation.7 | async-start | bytes 1310720 | tf_op jit(solution)/shard_map/all_gather | solution.py:153
  87.1 160.4 %all-gather.17.cloned.1.call-start = ((), (), s32[]{:S(2)}) async-start(), calls=%async_computation.6 | async-start | bytes 9437184 | tf_op jit(solution)/shard_map/all_gather | solution.py:161
  101.6 271.0 %all-gather.21.cloned.1.call-start = ((), (), s32[]{:S(2)}) async-start(), calls=%async_computation.8 | async-start | bytes 9437184 | tf_op jit(solution)/shard_map/all_gather | solution.py:162
  120.5 285.1 %all-gather.23.cloned.1.call-start = ((), (), s32[]{:S(2)}) async-start(), calls=%async_computation.9 | async-start | bytes 2621440 | tf_op jit(solution)/shard_map/all_gather | solution.py:136
  121.1 1.6 copy-start.32
  121.1 347.0 %all-gather.25.cloned.1.call-start = ((), (), s32[]{:S(2)}) async-start(), calls=%async_computation.10 | async-start | bytes 13434880 | tf_op jit(solution)/shard_map/all_gather | solution.py:174
  121.9 389.0 %all-gather.27.cloned.1.call-start = ((), (), s32[]{:S(2)}) async-start(), calls=%async_computation.11 | async-start | bytes 6717440 | tf_op jit(solution)/shard_map/all_gather | solution.py:175
  122.6 439.7 %all-gather.29.cloned.1.call-start = ((), (), s32[]{:S(2)}) async-start(), calls=%async_computation.12 | async-start | bytes 2359296 | tf_op jit(solution)/shard_map/all_gather | solution.py:234
  128.8 515.6 %all-gather.31.cloned.1.call-start = ((), (), s32[]{:S(2)}) async-start(), calls=%async_computation.13 | async-start | bytes 2359296 | tf_op jit(solution)/shard_map/all_gather | solution.py:235
  274.2 5.8 copy-start
  405.6 3.1 copy-start.19
  468.1 51.9 %slice-start = ((s8[10747904]{0:T(1024)(128)(4,1)}), s8[2359296]{0:T(1024)(128)(4,1)S(1)}, s32[]{:S(2)}) async-start(s8[10747904]{0:T(1024)(128)(4,1)} %bitcast.135), calls=%async_computation.20 | async-start | bytes 4718592
  510.8 8.2 copy-start.3
  510.8 9.1 slice-start.1
  510.8 9.1 slice-start.2
  519.9 5.7 copy-start.2
  519.9 6.0 copy-start.7
  529.5 2.3 copy-start.16
  529.5 3.5 copy-start.4
  534.5 4.2 copy-start.13
  534.5 214.8 %all-reduce.13.cloned.1.call-start = ((), (), s32[]{:S(2)}) async-start(), calls=%async_computation.18 | async-start | bytes 4194304
  567.0 10.1 copy-start.5
  567.1 10.1 copy-start.18
  578.3 34.2 %copy-start.21 = (f32[2,64,16,64]{1,3,2,0:T(8,128)S(1)}, f32[2,64,16,64]{1,3,2,0:T(8,128)}, u32[]{:S(2)}) copy-start(f32[2,64,16,64]{1,3,2,0:T(8,128)} %get-tuple-element.52) | copy-start | bytes 1572868
  612.5 31.9 %copy-start.11 = (bf16[2,64,16,64]{1,3,2,0:T(8,128)(2,1)}, bf16[2,64,16,64]{1,3,2,0:T(8,128)(2,1)S(1)}, u32[]{:S(2)}) copy-start(bf16[2,64,16,64]{1,3,2,0:T(8,128)(2,1)S(1)} %copy.113) | copy-start | bytes 786436
  662.5 132.9 %reduce-scatter.7.cloned.1.call-start = ((), (), s32[]{:S(2)}) async-start(), calls=%async_computation.15 | async-start | bytes 5242880 | tf_op jit(solution)/shard_map/reduce_scatter | solution.py:274
  668.9 1.1 copy-start.8
  669.0 197.1 %reduce-scatter.11.cloned.1.call-start = ((), (), s32[]{:S(2)}) async-start(), calls=%async_computation.17 | async-start | bytes 13434880 | tf_op jit(solution)/shard_map/reduce_scatter | solution.py:203
  676.5 0.7 copy-start.33
  676.5 291.1 %reduce-scatter.5.cloned.1.call-start = ((), (), s32[]{:S(2)}) async-start(), calls=%async_computation.14 | async-start | bytes 15728640 | tf_op jit(solution)/shard_map/reduce_scatter | solution.py:273
  747.1 3.7 copy-start.12
  767.7 1.2 copy-start.14
  767.8 1.3 copy-start.20
  770.7 3.6 copy-start.23
  780.7 345.9 %reduce-scatter.9.cloned.1.call-start = ((), (), s32[]{:S(2)}) async-start(), calls=%async_computation.16 | async-start | bytes 26869760 | tf_op jit(solution)/shard_map/reduce_scatter | solution.py:202
  795.3 728.5 %all-reduce.15.cloned.1.call-start = ((), (), s32[]{:S(2)}) async-start(), calls=%async_computation.19 | async-start | bytes 24510464 | tf_op jit(solution)/shard_map/psum | solution.py:276
  1126.6 2.1 copy-start.25
  1126.7 2.1 copy-start.27
  1128.7 5.2 copy-start.31
  1128.7 5.2 copy-start.29
  1128.8 34.8 %copy-start.6 = (f32[2,64,1024]{2,1,0:T(8,128)S(1)}, f32[2,64,1024]{2,1,0:T(8,128)}, u32[]{:S(2)}) copy-start(f32[2,64,1024]{2,1,0:T(8,128)} %get-tuple-element.38) | copy-start | bytes 1572868
  1128.8 34.8 %copy-start.17 = (bf16[2,64,1024]{2,1,0:T(8,128)(2,1)S(1)}, bf16[2,64,1024]{2,1,0:T(8,128)(2,1)}, u32[]{:S(2)}) copy-start(bf16[2,64,1024]{2,1,0:T(8,128)(2,1)} %param.15) | copy-start | bytes 786436
  1523.9 6.4 copy-start.10
  1530.2 3.7 copy-start.15
Sparse Core Ops, SparseCore 0:
  9.6 49.0 all-gather.12
  84.8 16.7 all-gather.14
  103.7 16.7 all-gather.18
  122.5 124.9 all-gather.16
  249.4 123.1 all-gather.20
  374.0 20.7 all-gather.22
  396.3 71.6 all-gather.24
  469.6 41.1 all-gather.26
  513.0 49.2 all-gather.28
  564.3 54.1 all-gather.30
  662.6 66.4 all-reduce.12
  732.2 44.1 reduce-scatter.6
  779.0 86.9 reduce-scatter.10
  868.5 99.0 reduce-scatter.4
  970.1 156.4 reduce-scatter.8
  1132.1 391.6 all-reduce.14
where the time goes:
time: 1550 us; the launch traced here: 1540 us
  waiting for transfers between devices  1100 us (71%)
  blocking collectives  161 us (10%)
  matrix products  131 us (8%)
  local copies, waits for them, and re-layouts  119 us (8%)
  other arithmetic  18.1 us (1%)
  between operations  16.3 us (1%)
    psum x1, waiting for transfers between devices, on_device(): lax.psum((gain_one_sum, gain_two_sum, proj_sum, out_sum), 'ctx')  359 us
    reduce_scatter x1, waiting for transfers between devices, on_device(): lax.psum_scatter(lift_grad, 'fsdp', scatter_dimension=0, tiled=True)  159 us
    all_gather x1, waiting for transfers between devices, on_device(): lax.all_gather(key_block, 'ctx', axis=1, tiled=True)  119 us
    reduce_scatter x1, waiting for transfers between devices, on_device(): lax.psum_scatter(proj_grad, 'fsdp', scatter_dimension=0, tiled=True)  102 us
    all_gather x1, waiting for transfers between devices, on_device(): lax.all_gather(value_block, 'ctx', axis=1, tiled=True)  92.6 us
    reduce_scatter x1, waiting for transfers between devices, on_device(): lax.psum_scatter(down_grad, 'fsdp', scatter_dimension=0, tiled=True)  70.6 us
    unnamed x2, blocking collectives  62.9 us
    all_gather x1, waiting for transfers between devices, on_device(): lax.all_gather(mlp_in, 'fsdp', axis=0, tiled=True)  59.4 us
  transfers between devices with their start and end apart: 16, of which 12 were waited for; matrix products, arithmetic and copies ran while one was open for 13% of the time, Pallas kernels for 0%

commit v1 on v0

--- a/solution.py
+++ b/solution.py
@@ -1,6 +1,10 @@
+import functools
+
 import jax
 import jax.numpy as jnp
 from jax import lax
+from jax.experimental import pallas as pl
+from jax.experimental.pallas import tpu as pltpu
 from jax.sharding import PartitionSpec as P
 
 HEADS = 16
@@ -120,34 +124,241 @@
     return (key_grad, value_grad)
 
 
-def on_device(inputs, attn_gain, attn_proj, attn_out, mlp_gain, mlp_in, mlp_out, cotangent):
-    seq_count, row_count, model_width = inputs.shape
-    head_size = HEAD_DIM
-    head_count = HEADS
-    scaling = head_size ** (-0.5)
-    fsdp_count = lax.axis_size("fsdp")
-    fsdp_place = lax.axis_index("fsdp")
-    start_row = (lax.axis_index("ctx") * fsdp_count + fsdp_place) * row_count
-    cos_table, sin_table = angles(start_row + jnp.arange(row_count, dtype=jnp.int32), head_size)
-    tokens = seq_count * row_count
-    gain_one, proj_full, out_full = (
-        lax.all_gather(attn_gain, "fsdp", axis=0, tiled=True),
-        lax.all_gather(attn_proj, "fsdp", axis=0, tiled=True),
-        lax.all_gather(attn_out, "fsdp", axis=0, tiled=True),
-    )
-    states = inputs.astype(jnp.float32)
-    normed, norm_back_one = jax.vjp(layer_norm, states, gain_one.astype(jnp.float32))
-    normed_low = normed.astype(jnp.bfloat16).reshape(tokens, model_width)
-    mixed_rows = jnp.dot(normed_low, proj_full, preferred_element_type=jnp.float32).reshape(
-        seq_count, row_count, 3, head_count, head_size
-    )
+MESH_ID = pl.DeviceIdType.MESH
+
+
+def exchange_kernel(ctx_count, fsdp_count, x_ref, o_ref, send_sem, recv_sem, own_sem):
+    count = ctx_count * fsdp_count
+    me = lax.axis_index("ctx") * fsdp_count + lax.axis_index("fsdp")
+    barrier = pltpu.get_barrier_semaphore()
+
+    def target(step):
+        place = lax.rem(me + step, count)
+        return place, (place // fsdp_count, lax.rem(place, fsdp_count))
+
+    def copy_to(step):
+        place, device = target(step)
+        return pltpu.make_async_remote_copy(
+            src_ref=x_ref.at[place],
+            dst_ref=o_ref.at[me],
+            send_sem=send_sem.at[step],
+            recv_sem=recv_sem.at[step],
+            device_id=device,
+            device_id_type=MESH_ID,
+        )
+
+    @pl.loop(1, count)
+    def _(step):
+        pl.semaphore_signal(barrier, inc=1, device_id=target(step)[1], device_id_type=MESH_ID)
+
+    pl.semaphore_wait(barrier, count - 1)
+    own = pltpu.make_async_copy(x_ref.at[me], o_ref.at[me], own_sem)
+    own.start()
+
+    @pl.loop(1, count)
+    def _(step):
+        copy_to(step).start()
+
+    own.wait()
+
+    @pl.loop(1, count)
+    def _(step):
+        copy_to(step).wait()
+
+
+def exchange(blocks, ctx_count, fsdp_count, collective_id):
+    count = ctx_count * fsdp_count
+    return pl.pallas_call(
+        functools.partial(exchange_kernel, ctx_count, fsdp_count),
+        out_shape=jax.ShapeDtypeStruct(blocks.shape, blocks.dtype),
+        in_specs=[pl.BlockSpec(memory_space=pl.ANY)],
+        out_specs=pl.BlockSpec(memory_space=pl.ANY),
+        scratch_shapes=[
+            pltpu.SemaphoreType.DMA((count,)),
+            pltpu.SemaphoreType.DMA((count,)),
+            pltpu.SemaphoreType.DMA,
+        ],
+        compiler_params=pltpu.CompilerParams(collective_id=collective_id, has_side_effects=True),
+    )(blocks)
+
+
+def pack(blocks):
+    half = blocks.shape[-2] // 2
+    return jnp.concatenate([blocks[..., :half, :], blocks[..., half:, :]], axis=-1)
+
+
+def unpack(blocks):
+    half = blocks.shape[-1] // 2
+    return jnp.concatenate([blocks[..., :half], blocks[..., half:]], axis=-2)
+
+
+CONTRACT_LAST = (((1,), (1,)), ((), ()))
+CONTRACT_FIRST = (((0,), (0,)), ((), ()))
+
+
+def attend_kernel(q_ref, k_ref, v_ref, context_ref, log_ref):
+    scores = lax.dot_general(
+        q_ref[...], k_ref[...], CONTRACT_LAST, preferred_element_type=jnp.float32
+    )
+    top = jnp.max(scores, axis=-1, keepdims=True)
+    weights = jnp.exp(scores - top)
+    total = jnp.sum(weights, axis=-1, keepdims=True)
+    weighted = jnp.dot(
+        weights.astype(jnp.bfloat16), v_ref[...], preferred_element_type=jnp.float32
+    )
+    context_ref[...] = weighted / total
+    log_ref[...] = top + jnp.log(total)
+
+
+def attend(queries, key_rows, value_rows, block):
+    rows, size = queries.shape
+    return pl.pallas_call(
+        attend_kernel,
+        grid=(rows // block,),
+        out_shape=(
+            jax.ShapeDtypeStruct((rows, size), jnp.float32),
+            jax.ShapeDtypeStruct((rows, 1), jnp.float32),
+        ),
+        in_specs=[
+            pl.BlockSpec((block, size), lambda i: (i, 0)),
+            pl.BlockSpec((rows, size), lambda i: (0, 0)),
+            pl.BlockSpec((rows, size), lambda i: (0, 0)),
+        ],
+        out_specs=(
+            pl.BlockSpec((block, size), lambda i: (i, 0)),
+            pl.BlockSpec((block, 1), lambda i: (i, 0)),
+        ),
+        compiler_params=pltpu.CompilerParams(vmem_limit_bytes=48 * 1024 * 1024),
+    )(queries, key_rows, value_rows)
+
+
+def attend_back_kernel(
+    q_ref, k_ref, v_ref, context_ref, log_ref, grad_ref, dq_ref, dk_ref, dv_ref
+):
+    @pl.when(pl.program_id(0) == 0)
+    def _():
+        dk_ref[...] = jnp.zeros_like(dk_ref)
+        dv_ref[...] = jnp.zeros_like(dv_ref)
+
+    grad = grad_ref[...]
+    inner = jnp.sum(grad.astype(jnp.float32) * context_ref[...], axis=-1, keepdims=True)
+    scores = lax.dot_general(
+        q_ref[...], k_ref[...], CONTRACT_LAST, preferred_element_type=jnp.float32
+    )
+    probs = jnp.exp(scores - log_ref[...])
+    prob_grad = lax.dot_general(
+        grad, v_ref[...], CONTRACT_LAST, preferred_element_type=jnp.float32
+    )
+    score_grad = (probs * (prob_grad - inner)).astype(jnp.bfloat16)
+    dv_ref[...] += lax.dot_general(
+        probs.astype(jnp.bfloat16), grad, CONTRACT_FIRST, preferred_element_type=jnp.float32
+    )
+    dk_ref[...] += lax.dot_general(
+        score_grad, q_ref[...], CONTRACT_FIRST, preferred_element_type=jnp.float32
+    )
+    dq_ref[...] = jnp.dot(score_grad, k_ref[...], preferred_element_type=jnp.float32)
+
+
+def attend_back(queries, key_rows, value_rows, context, log_total, grad, block):
+    rows, size = queries.shape
+    part = pl.BlockSpec((block, size), lambda i: (i, 0))
+    whole = pl.BlockSpec((rows, size), lambda i: (0, 0))
+    return pl.pallas_call(
+        attend_back_kernel,
+        grid=(rows // block,),
+        out_shape=(jax.ShapeDtypeStruct((rows, size), jnp.float32),) * 3,
+        in_specs=[
+            part,
+            whole,
+            whole,
+            part,
+            pl.BlockSpec((block, 1), lambda i: (i, 0)),
+            part,
+        ],
+        out_specs=(part, whole, whole),
+        compiler_params=pltpu.CompilerParams(vmem_limit_bytes=48 * 1024 * 1024),
+    )(queries, key_rows, value_rows, context, log_total, grad)
+
+
+def by_head_forward(mixed_rows, cos_table, sin_table, scaling):
+    seq_count, row_count, _, head_count, head_size = mixed_rows.shape
+    ctx_count, fsdp_count = lax.axis_size("ctx"), lax.axis_size("fsdp")
+    count = ctx_count * fsdp_count
+    queries = rotate(mixed_rows[:, :, 0], cos_table, sin_table).astype(jnp.bfloat16) * scaling
+    key_rows = rotate(mixed_rows[:, :, 1], cos_table, sin_table).astype(jnp.bfloat16)
+    value_rows = mixed_rows[:, :, 2].astype(jnp.bfloat16)
+    to_head = lambda rows: rows.transpose(0, 2, 1, 3).reshape(count, row_count, head_size)
+    sent = jnp.concatenate(
+        [
+            jnp.concatenate([to_head(queries), to_head(key_rows)], axis=-1),
+            pack(to_head(value_rows)),
+        ],
+        axis=1,
+    )
+    got = exchange(sent, ctx_count, fsdp_count, 1)
+    flat = lambda rows: rows.reshape(count * row_count, head_size)
+    queries = flat(got[:, :row_count, :head_size])
+    key_rows = flat(got[:, :row_count, head_size:])
+    value_rows = flat(unpack(got[:, row_count:]))
+    context, log_total = attend(queries, key_rows, value_rows, 256)
+    back = exchange(
+        pack(context.astype(jnp.bfloat16).reshape(count, row_count, head_size)),
+        ctx_count,
+        fsdp_count,
+        2,
+    )
+    context_low = (
+        unpack(back)
+        .reshape(seq_count, head_count, row_count, head_size)
+        .transpose(0, 2, 1, 3)
+        .reshape(seq_count * row_count, head_count * head_size)
+    )
+    return context_low, (queries, key_rows, value_rows, context, log_total)
+
+
+def by_head_back(context_grad, saved, scaling):
+    seq_count, row_count, head_count, head_size = context_grad.shape
+    ctx_count, fsdp_count = lax.axis_size("ctx"), lax.axis_size("fsdp")
+    count = ctx_count * fsdp_count
+    queries, key_rows, value_rows, context, log_total = saved
+    sent = pack(context_grad.transpose(0, 2, 1, 3).reshape(count, row_count, head_size))
+    grad = unpack(exchange(sent, ctx_count, fsdp_count, 3)).reshape(count * row_count, head_size)
+    query_grad, key_grad, value_grad = attend_back(
+        queries, key_rows, value_rows, context, log_total, grad, 256
+    )
+    cos_all, sin_all = angles(jnp.arange(count * row_count, dtype=jnp.int32), head_size)
+    cos_all, sin_all = cos_all[:, 0], sin_all[:, 0]
+    query_pre = unrotate(query_grad * scaling, cos_all, sin_all).astype(jnp.bfloat16)
+    key_pre = unrotate(key_grad, cos_all, sin_all).astype(jnp.bfloat16)
+    split = lambda rows: rows.reshape(count, row_count, head_size)
+    sent = jnp.concatenate(
+        [
+            jnp.concatenate([split(query_pre), split(key_pre)], axis=-1),
+            pack(split(value_grad.astype(jnp.bfloat16))),
+        ],
+        axis=1,
+    )
+    got = exchange(sent, ctx_count, fsdp_count, 4)
+    parts = jnp.stack(
+        [got[:, :row_count, :head_size], got[:, :row_count, head_size:], unpack(got[:, row_count:])]
+    )
+    return (
+        parts.reshape(3, seq_count, head_count, row_count, head_size)
+        .transpose(1, 3, 0, 2, 4)
+        .reshape(seq_count * row_count, 3 * head_count * head_size)
+    )
+
+
+def by_block_forward(mixed_rows, cos_table, sin_table, scaling):
+    seq_count, row_count, _, head_count, head_size = mixed_rows.shape
+    width = head_count * head_size
     queries = rotate(mixed_rows[:, :, 0], cos_table, sin_table).astype(jnp.bfloat16)
     key_flat = (
         rotate(mixed_rows[:, :, 1], cos_table, sin_table)
         .astype(jnp.bfloat16)
-        .reshape(seq_count, row_count, model_width)
-    )
-    value_flat = mixed_rows[:, :, 2].astype(jnp.bfloat16).reshape(seq_count, row_count, model_width)
+        .reshape(seq_count, row_count, width)
+    )
+    value_flat = mixed_rows[:, :, 2].astype(jnp.bfloat16).reshape(seq_count, row_count, width)
     key_block, value_block = (
         lax.all_gather(key_flat, "fsdp", axis=1, tiled=True),
         lax.all_gather(value_flat, "fsdp", axis=1, tiled=True),
@@ -164,17 +375,108 @@
     )
     context = (weighted / denominator[..., None]).transpose(0, 2, 1, 3)
     log_total = running_max + jnp.log(denominator)
-    context_low = context.reshape(tokens, model_width).astype(jnp.bfloat16)
+    context_low = context.reshape(seq_count * row_count, width).astype(jnp.bfloat16)
+    return context_low, (queries, key_block, value_block, context, log_total, cos_table, sin_table)
+
+
+def by_block_back(context_grad, saved, scaling):
+    seq_count, row_count, head_count, head_size = context_grad.shape
+    width = head_count * head_size
+    queries, key_block, value_block, context, log_total, cos_table, sin_table = saved
+    inner = jnp.sum(context_grad.astype(jnp.float32) * context, axis=-1)
+    inner_heads = inner.transpose(0, 2, 1)
+    log_rows = log_total.transpose(0, 2, 1)
+    query_grad = query_step(
+        queries,
+        context_grad,
+        log_total,
+        inner_heads,
+        scaling,
+        (
+            lax.all_gather(key_block, "ctx", axis=1, tiled=True),
+            lax.all_gather(value_block, "ctx", axis=1, tiled=True),
+        ),
+    )
+    block_len = key_block.shape[1]
+    query_wide = queries.reshape(seq_count, row_count, width).astype(jnp.float32)
+    grad_wide = context_grad.reshape(seq_count, row_count, width).astype(jnp.float32)
+    key_grad, value_grad = key_step(
+        as_heads(key_block, head_size),
+        as_heads(value_block, head_size),
+        scaling,
+        (
+            lax.all_gather(query_wide, "ctx", axis=1, tiled=True),
+            lax.all_gather(grad_wide, "ctx", axis=1, tiled=True),
+            lax.all_gather(log_rows, "ctx", axis=1, tiled=True),
+            lax.all_gather(inner, "ctx", axis=1, tiled=True),
+        ),
+    )
+    own = lambda grad: lax.psum_scatter(
+        grad.reshape(seq_count, block_len, width), "fsdp", scatter_dimension=1, tiled=True
+    ).reshape(seq_count, row_count, head_count, head_size)
+    query_pre = unrotate(query_grad * scaling, cos_table, sin_table)
+    key_pre = unrotate(own(key_grad) * scaling, cos_table, sin_table)
+    return (
+        jnp.stack([query_pre, key_pre, own(value_grad)], axis=2)
+        .reshape(seq_count * row_count, 3 * width)
+        .astype(jnp.bfloat16)
+    )
+
+
+def group_rows(rows):
+    return lax.all_gather(rows, "fsdp", axis=0, tiled=True)
+
+
+def group_columns(rows):
+    return lax.all_to_all(rows, "fsdp", split_axis=1, concat_axis=0, tiled=True)
+
+
+def weight_grad(left, right):
+    return jnp.einsum("tw,tf->wf", left, right, preferred_element_type=jnp.float32)
+
+
+def sum_blocks(grads):
+    low = lax.psum(tuple(grad.astype(jnp.bfloat16) for grad in grads), "ctx")
+    return tuple(grad.astype(jnp.float32) for grad in low)
+
+
+def on_device(inputs, attn_gain, attn_proj, attn_out, mlp_gain, mlp_in, mlp_out, cotangent):
+    seq_count, row_count, model_width = inputs.shape
+    head_size = HEAD_DIM
+    head_count = HEADS
+    scaling = head_size ** (-0.5)
+    fsdp_count = lax.axis_size("fsdp")
+    fsdp_place = lax.axis_index("fsdp")
+    device_count = lax.axis_size("ctx") * fsdp_count
+    one_head_each = device_count == seq_count * head_count
+    start_row = (lax.axis_index("ctx") * fsdp_count + fsdp_place) * row_count
+    cos_table, sin_table = angles(start_row + jnp.arange(row_count, dtype=jnp.int32), head_size)
+    tokens = seq_count * row_count
+    gains = lax.all_gather(jnp.stack([attn_gain, mlp_gain]), "fsdp", axis=1, tiled=True).astype(
+        jnp.float32
+    )
+    gain_one, gain_two = gains[0], gains[1]
+    proj_full, out_full, lift_full, down_full = (
+        lax.all_gather(attn_proj, "fsdp", axis=0, tiled=True),
+        lax.all_gather(attn_out, "fsdp", axis=0, tiled=True),
+        lax.all_gather(mlp_in, "fsdp", axis=0, tiled=True),
+        lax.all_gather(mlp_out, "fsdp", axis=0, tiled=True),
+    )
+    states = inputs.astype(jnp.float32)
+    normed, norm_back_one = jax.vjp(layer_norm, states, gain_one)
+    normed_low = normed.astype(jnp.bfloat16).reshape(tokens, model_width)
+    mixed_rows = jnp.dot(normed_low, proj_full, preferred_element_type=jnp.float32).reshape(
+        seq_count, row_count, 3, head_count, head_size
+    )
+    attention, attention_back = (
+        (by_head_forward, by_head_back) if one_head_each else (by_block_forward, by_block_back)
+    )
+    context_low, saved = attention(mixed_rows, cos_table, sin_table, scaling)
     branch = jnp.dot(context_low, out_full, preferred_element_type=jnp.float32).reshape(
         seq_count, row_count, model_width
     )
     middle = states + branch
-    gain_two, lift_full, down_full = (
-        lax.all_gather(mlp_gain, "fsdp", axis=0, tiled=True),
-        lax.all_gather(mlp_in, "fsdp", axis=0, tiled=True),
-        lax.all_gather(mlp_out, "fsdp", axis=0, tiled=True),
-    )
-    normed_two, norm_back_two = jax.vjp(layer_norm, middle, gain_two.astype(jnp.float32))
+    normed_two, norm_back_two = jax.vjp(layer_norm, middle, gain_two)
     normed_two_low = normed_two.astype(jnp.bfloat16).reshape(tokens, model_width)
     lifted = jnp.dot(normed_two_low, lift_full, preferred_element_type=jnp.float32)
     gate_out, gated_back = jax.vjp(gated_unit, lifted)
@@ -193,90 +495,37 @@
     ).reshape(seq_count, row_count, model_width)
     middle_part, gain_two_grad = norm_back_two(normed_two_grad)
     middle_grad = cotangent.astype(jnp.float32) + middle_part
-    down_grad = jnp.einsum("tf,td->fd", gate_low, seed_rows, preferred_element_type=jnp.float32)
-    lift_grad = jnp.einsum(
-        "tw,tf->wf", normed_two_low, lifted_grad, preferred_element_type=jnp.float32
-    )
-    gain_two_sum, lift_sum, down_sum = (
-        lax.psum_scatter(gain_two_grad, "fsdp", scatter_dimension=0, tiled=True),
-        lax.psum_scatter(lift_grad, "fsdp", scatter_dimension=0, tiled=True),
-        lax.psum_scatter(down_grad, "fsdp", scatter_dimension=0, tiled=True),
-    )
-    lift_sum, down_sum = lax.psum((lift_sum, down_sum), "ctx")
     middle_low = middle_grad.reshape(tokens, model_width).astype(jnp.bfloat16)
     context_grad = (
         jnp.einsum("tv,wv->tw", middle_low, out_full, preferred_element_type=jnp.float32)
         .astype(jnp.bfloat16)
         .reshape(seq_count, row_count, head_count, head_size)
     )
-    inner = jnp.sum(context_grad.astype(jnp.float32) * context, axis=-1)
-    inner_heads = inner.transpose(0, 2, 1)
-    log_rows = log_total.transpose(0, 2, 1)
-    query_grad = query_step(
-        queries,
-        context_grad,
-        log_total,
-        inner_heads,
-        scaling,
-        (
-            lax.all_gather(key_block, "ctx", axis=1, tiled=True),
-            lax.all_gather(value_block, "ctx", axis=1, tiled=True),
-        ),
-    )
-    block_len = key_block.shape[1]
-    query_wide = queries.reshape(seq_count, row_count, model_width).astype(jnp.float32)
-    grad_wide = context_grad.reshape(seq_count, row_count, model_width).astype(jnp.float32)
-    key_grad, value_grad = key_step(
-        as_heads(key_block, head_size),
-        as_heads(value_block, head_size),
-        scaling,
-        (
-            lax.all_gather(query_wide, "ctx", axis=1, tiled=True),
-            lax.all_gather(grad_wide, "ctx", axis=1, tiled=True),
-            lax.all_gather(log_rows, "ctx", axis=1, tiled=True),
-            lax.all_gather(inner, "ctx", axis=1, tiled=True),
-        ),
-    )
-    key_own, value_own = (
-        lax.psum_scatter(
-            key_grad.reshape(seq_count, block_len, model_width),
-            "fsdp",
-            scatter_dimension=1,
-            tiled=True,
-        ),
-        lax.psum_scatter(
-            value_grad.reshape(seq_count, block_len, model_width),
-            "fsdp",
-            scatter_dimension=1,
-            tiled=True,
-        ),
-    )
-    query_pre = unrotate(query_grad * scaling, cos_table, sin_table)
-    key_pre = unrotate(
-        key_own.reshape(seq_count, row_count, head_count, head_size) * scaling, cos_table, sin_table
-    )
-    value_pre = value_own.reshape(seq_count, row_count, head_count, head_size)
-    mixed_grad = (
-        jnp.stack([query_pre, key_pre, value_pre], axis=2)
-        .reshape(tokens, 3 * model_width)
-        .astype(jnp.bfloat16)
-    )
+    lift_grad = weight_grad(group_columns(normed_two_low), group_rows(lifted_grad))
+    down_grad = weight_grad(group_columns(gate_low), group_rows(seed_rows))
+    out_grad = weight_grad(group_columns(context_low), group_rows(middle_low))
+    lift_sum, down_sum, out_sum = sum_blocks((lift_grad, down_grad, out_grad))
+    mixed_grad = attention_back(context_grad, saved, scaling)
     normed_grad = jnp.einsum(
         "tm,wm->tw", mixed_grad, proj_full, preferred_element_type=jnp.float32
     ).reshape(seq_count, row_count, model_width)
     state_part, gain_one_grad = norm_back_one(normed_grad)
     input_grad = middle_grad + state_part
-    out_grad = jnp.einsum("tw,tv->wv", context_low, middle_low, preferred_element_type=jnp.float32)
-    proj_grad = jnp.einsum("tw,tm->wm", normed_low, mixed_grad, preferred_element_type=jnp.float32)
-    gain_one_sum, proj_sum, out_sum = (
-        lax.psum_scatter(gain_one_grad, "fsdp", scatter_dimension=0, tiled=True),
-        lax.psum_scatter(proj_grad, "fsdp", scatter_dimension=0, tiled=True),
-        lax.psum_scatter(out_grad, "fsdp", scatter_dimension=0, tiled=True),
-    )
-    gain_one_sum, gain_two_sum, proj_sum, out_sum = lax.psum(
-        (gain_one_sum, gain_two_sum, proj_sum, out_sum), "ctx"
-    )
-    return (outputs, input_grad, gain_one_sum, proj_sum, out_sum, gain_two_sum, lift_sum, down_sum)
+    proj_grad = weight_grad(group_columns(normed_low), group_rows(mixed_grad))
+    (proj_sum,) = sum_blocks((proj_grad,))
+    gain_sums = lax.psum(jnp.stack([gain_one_grad, gain_two_grad]), ("ctx", "fsdp"))
+    gain_width = attn_gain.shape[0]
+    gain_own = lax.dynamic_slice_in_dim(gain_sums, fsdp_place * gain_width, gain_width, axis=1)
+    return (
+        outputs,
+        input_grad,
+        gain_own[0],
+        proj_sum,
+        out_sum,
+        gain_own[1],
+        lift_sum,
+        down_sum,
+    )
 
 
 def solution(mesh):

time: 1550 us -> 635 us (0.41)
  waiting for transfers between devices: 1100 us -> 317 us
  blocking collectives: 161 us -> 51.2 us
  Pallas kernels: 0 us -> 87.1 us
  local copies, waits for them, and re-layouts: 119 us -> 41.7 us
  matrix products: 131 us -> 55.7 us
  other arithmetic: 18.1 us -> 45.9 us
    reduce_scatter x4 -> x0, waiting for transfers between devices: 331 us -> none  [the longest x1 159 us: on_device(): lax.psum_scatter(lift_grad, 'fsdp', scatter_dimension=0, tiled=True)]
    all_gather x6 -> x4, waiting for transfers between devices: 266 us -> 35.3 us  [group_rows(): return lax.all_gather(rows, 'fsdp', axis=0, tiled=True)]
    psum x1, waiting for transfers between devices: 359 us -> 161 us  [sum_blocks(): low = lax.psum(tuple((grad.astype(jnp.bfloat16) for grad in grads)), 'ctx')]
    pallas_call x0 -> x6, Pallas kernels: none -> 87.1 us  [the longest x4 64.5 us: exchange(): pl.pallas_call(functools.partial(exchange_kernel, ctx_count, fsdp_count),...]
    dot_general x10 -> x4, matrix products: 92.6 us -> 15.6 us  [weight_grad(): jnp.einsum('tw,tf->wf', left, right, preferred_element_type=jnp.float32)]
    all_gather x4 -> x1, blocking collectives: 74.8 us -> 5.98 us  [on_device(): lax.all_gather(jnp.stack([attn_gain, mlp_gain]), 'fsdp', axis=1, tiled=True)]
    unnamed x2 -> x0, blocking collectives: 62.9 us -> none
    all_gather x4 -> x0, local copies, waits for them, and re-layouts: 48.9 us -> none  [the longest x1 21.3 us: on_device(): lax.all_gather(key_block, 'ctx', axis=1, tiled=True)]
  transfers between devices with their start and end apart: 16 -> 13, of which waited for: 12 -> 9; matrix products, arithmetic and copies ran while one was open for 13% -> 20% of each run, Pallas kernels for 0% -> 14%
where the time goes in v1:
time: 635 us; the launch traced here: 629 us
  waiting for transfers between devices  317 us (50%)
  Pallas kernels  87.1 us (14%)
  matrix products  55.7 us (9%)
  blocking collectives  51.2 us (8%)
  other arithmetic  45.9 us (7%)
  local copies, waits for them, and re-layouts  41.7 us (7%)
  starting transfers between devices  15.1 us (2%)
  between operations  14.9 us (2%)
    psum x1, waiting for transfers between devices, sum_blocks(): low = lax.psum(tuple((grad.astype(jnp.bfloat16) for grad in grads)), 'ctx')  161 us
    pallas_call x4, Pallas kernels, exchange(): pl.pallas_call(functools.partial(exchange_kernel, ctx_count, fsdp_count),...  64.5 us
    psum x1, blocking collectives, on_device(): lax.psum(jnp.stack([gain_one_grad, gain_two_grad]), ('ctx', 'fsdp'))  45.2 us
    all_gather x1, waiting for transfers between devices, on_device(): lax.all_gather(attn_proj, 'fsdp', axis=0, tiled=True)  39.3 us
    all_gather x4, waiting for transfers between devices, group_rows(): return lax.all_gather(rows, 'fsdp', axis=0, tiled=True)  35.3 us
    all_gather x1, waiting for transfers between devices, on_device(): lax.all_gather(mlp_out, 'fsdp', axis=0, tiled=True)  32.7 us
    all_gather x1, waiting for transfers between devices, on_device(): lax.all_gather(mlp_in, 'fsdp', axis=0, tiled=True)  26.4 us
    all_to_all x4, waiting for transfers between devices, group_columns(): return lax.all_to_all(rows, 'fsdp', split_axis=1, concat_axis=0, tiled=True)  18.5 us
  transfers between devices with their start and end apart: 13, of which 9 were waited for; matrix products, arithmetic and copies ran while one was open for 20% of the time, Pallas kernels for 14%

profile of v1, /device:TPU:0, one launch (start us, length us, event | category | flops | bytes accessed | tf_op | source)
XLA Modules:
  0.0 628.6 jit_solution(5711606774770166298)
XLA Ops:
  10.7 6.0 all_gather.27
  17.2 1.3 broadcast_multiply_fusion
  19.5 39.3 %all-gather.9.cloned.1.call-done = bf16[1024,3072]{1,0:T(8,128)(2,1)} async-done(((bf16[256,3072]{1,0:T(8,128)(2,1)}), bf16[1024,3072]{1,0:T(8,128)(2,1)}) %all-gather.9.cloned.1.call-update) | async-done | bytes 6291472 | tf_op jit(solution)/shard_map/all_gather | solution.py:460
  58.7 8.7 %copy.43 = bf16[3072,1024]{1,0:T(8,128)(2,1)} copy(bf16[3072,1024]{0,1:T(8,128)(2,1)} %bitcast.128) | data formatting | bytes 12582912 | tf_op jit(solution)/shard_map/dot_general | solution.py:468
  67.4 4.7 fusion.41
  73.0 1.4 slice_bitcast_fusion.1
  74.5 2.0 copy.47
  76.5 1.9 fusion.58
  78.4 2.4 slice_negate_fusion.2
  81.9 2.0 copy.46
  83.9 2.2 fusion.37
  86.1 1.4 copy.45
  87.5 2.3 maximum_maximum_fusion.x_ref
  89.9 18.3 %shard_map.143 = bf16[32,96,128]{2,1,0:T(8,128)(2,1)} custom-call(bf16[32,96,128]{2,1,0:T(8,128)(2,1)} %maximum_maximum_fusion.x_ref), custom_call_target="tpu_custom_call" | custom-call | tf_op jit(solution)/shard_map/pallas_call | solution.py:171
  108.1 1.5 fusion.54
  110.0 8.5 %shard_map.144 = (f32[2048,64]{1,0:T(8,128)S(1)}, f32[2048,1]{1,0:T(8,128)S(1)}) custom-call(bf16[2048,64]{1,0:T(8,128)(2,1)S(1)} %bitcast.125, bf16[2048,64]{1,0:T(8,128)(2,1)S(1)} %bitcast.123, bf16[2048,64]{1,0:T(8,128)(2,1)S(1)} %bitcast.121), custom_call_target="tpu_custom_call" | custom-call | tf_op jit(solution)/shard_map/pallas_call | solution.py:215
  120.5 15.6 %shard_map.145 = bf16[32,32,128]{2,1,0:T(8,128)(2,1)} custom-call(bf16[32,32,128]{2,1,0:T(8,128)(2,1)} %pad_maximum_fusion.5.x_ref), custom_call_target="tpu_custom_call" | custom-call | tf_op jit(solution)/shard_map/pallas_call | solution.py:171
  136.1 1.2 fusion.60
  138.6 2.1 fusion.63
  141.1 26.4 %all-gather.13.cloned.1.call-done = bf16[1024,5248]{1,0:T(8,128)(2,1)} async-done(((bf16[256,5248]{1,0:T(8,128)(2,1)}), bf16[1024,5248]{1,0:T(8,128)(2,1)}) %all-gather.13.cloned.1.call-update) | async-done | bytes 10747920 | tf_op jit(solution)/shard_map/all_gather | solution.py:462
  167.4 7.2 %fusion.64 = f32[128,5248]{1,0:T(8,128)} fusion(bf16[128,1024]{1,0:T(8,128)(2,1)S(1)} %bitcast.133, bf16[1024,5248]{1,0:T(8,128)(2,1)} %all-gather.13.cloned.1.call-done), kind=kOutput, calls=%fused_computation.130 | convolution fusion | flops 1375731712 | bytes 13697024 | tf_op jit(solution)/shard_map/dot_general | solution.py:481
  174.7 32.7 %all-gather.15.cloned.1.call-done = bf16[2624,1024]{1,0:T(8,128)(2,1)} async-done(((bf16[656,1024]{1,0:T(8,128)(2,1)}), bf16[2624,1024]{1,0:T(8,128)(2,1)}) %all-gather.15.cloned.1.call-update) | async-done | bytes 5373968 | tf_op jit(solution)/shard_map/all_gather | solution.py:463
  207.4 7.0 %fusion.39 = (f32[128,2624]{1,0:T(8,128)S(1)}, f32[128,2624]{1,0:T(8,128)S(1)}, f32[128,2624]{1,0:T(8,128)S(1)}) fusion(f32[128,5248]{1,0:T(8,128)} %fusion.64, bf16[128,1024]{1,0:T(8,128)(2,1)S(1)} %bitcast.138, bf16[2624,1024]{1,0:T(8,128)(2,1)} %all-gather.15.cloned.1.call-done), kind=kOutput, calls=%fused_computation.88 | convolution fusion | flops 709697536 | bytes 11010048 | tf_op jit(solution)/shard_map/td,fd->tf/dot_general | solution.py:491
  215.2 1.3 add_convert_fusion
  216.6 8.0 %fusion.66 = f32[128,1024]{1,0:T(8,128)S(1)} fusion(bf16[128,5248]{1,0:T(8,128)(2,1)} %add_convert_fusion, bf16[1024,5248]{1,0:T(8,128)(2,1)} %all-gather.13.cloned.1.call-done), kind=kOutput, calls=%fused_computation.132 | convolution fusion | flops 1375731712 | bytes 12615680 | tf_op jit(solution)/shard_map/tf,wf->tw/dot_general | solution.py:493
  224.9 3.4 fusion.65
  229.5 2.5 convolution_convert_fusion.4
  232.0 1.1 reshape.247
  233.2 1.4 copy.51
  235.5 10.9 %shard_map.146 = bf16[32,32,128]{2,1,0:T(8,128)(2,1)} custom-call(bf16[32,32,128]{2,1,0:T(8,128)(2,1)} %pad_maximum_fusion.6.x_ref), custom_call_target="tpu_custom_call" | custom-call | tf_op jit(solution)/shard_map/pallas_call | solution.py:171
  246.3 1.2 fusion.59
  247.7 14.1 %shard_map.147 = (f32[2048,64]{1,0:T(8,128)S(1)}, f32[2048,64]{1,0:T(8,128)S(1)}, f32[2048,64]{1,0:T(8,128)S(1)}) custom-call(bf16[2048,64]{1,0:T(8,128)(2,1)S(1)} %bitcast.126, bf16[2048,64]{1,0:T(8,128)(2,1)S(1)} %bitcast.124, bf16[2048,64]{1,0:T(8,128)(2,1)S(1)} %bitcast.122, f32[2048,64]{1,0:T(8,128)} %copy-done, f32[2048,1]{1,0:T(8,128)} %copy-done.1, ...), custom_call_target="tpu_custom_call" | custom-call | tf_op jit(solution)/shard_map/pallas_call | solution.py:266
  261.8 1.2 copy-done.2
  263.0 3.8 multiply_multiply_fusion.5
  267.2 5.5 fusion.18
  272.7 1.7 fusion.50
  274.4 1.2 copy-done.11
  275.6 5.1 fusion.19
  280.7 1.3 maximum_maximum_fusion.1.x_ref
  282.1 19.8 %shard_map.148 = bf16[32,96,128]{2,1,0:T(8,128)(2,1)} custom-call(bf16[32,96,128]{2,1,0:T(8,128)(2,1)} %maximum_maximum_fusion.1.x_ref), custom_call_target="tpu_custom_call" | custom-call | tf_op jit(solution)/shard_map/pallas_call | solution.py:171
  301.8 1.2 fusion.52
  304.9 1.9 reshape.253
  307.9 1.1 copy.58
  309.0 4.3 all-to-all-start.3
  314.2 1.7 copy.55
  317.8 7.4 %all-to-all-done.3 = bf16[128,4,656]{0,2,1:T(8,128)(2,1)} async-done(((bf16[128,4,656]{0,2,1:T(8,128)(2,1)}), bf16[128,4,656]{0,2,1:T(8,128)(2,1)}, u32[]{:S(2)}, u32[]{:S(2)}) %all-to-all-start.3) | async-done | bytes 671776 | tf_op jit(solution)/shard_map/all_to_all | solution.py:431
  325.3 3.4 all-to-all-start.1
  328.7 3.4 convolution_convert_fusion.2
  332.1 5.7 all-to-all-done.1
  337.8 3.4 all-to-all-start
  341.3 2.5 convolution_convert_fusion.3
  343.8 3.4 all-to-all-done
  347.3 3.7 all-to-all-start.2
  351.0 4.0 convolution_convert_fusion.1
  355.0 1.9 all-to-all-done.2
  356.9 35.3 %all-gather.21.cloned.1.call-done = bf16[512,5248]{1,0:T(8,128)(2,1)} async-done(((bf16[128,5248]{1,0:T(8,128)(2,1)}), bf16[512,5248]{1,0:T(8,128)(2,1)}) %all-gather.21.cloned.1.call-update) | async-done | bytes 5373968 | tf_op jit(solution)/shard_map/all_gather | solution.py:427
  392.2 5.7 convolution_convert_fusion
  397.9 1.1 dot_general.54
  399.0 5.1 fusion.34
  404.5 45.2 %psum.35 = f32[2,1024]{1,0:T(2,128)S(1)} all-reduce(f32[2,1024]{1,0:T(2,128)S(1)} %pad_maximum_fusion.8), channel_id=1, replica_groups=mesh['ctx'=8,'fsdp'=4] {'ctx','fsdp'}, use_global_device_ids=true, to_apply=%region_10.0 | all-reduce | flops 2048 | bytes 16384 | tf_op jit(solution)/shard_map/psum | solution.py:516
  451.4 161.0 %all-reduce.5.cloned.1.call-done = (bf16[256,3072]{1,0:T(8,128)(2,1)}, bf16[256,1024]{1,0:T(8,128)(2,1)}, bf16[256,5248]{1,0:T(8,128)(2,1)}, bf16[656,1024]{1,0:T(8,128)(2,1)}) async-done(((bf16[256,3072]{1,0:T(8,128)(2,1)}, bf16[256,1024]{1,0:T(8,128)(2,1)}, bf16[256,5248]{1,0:T(8,128)(2,1)}, bf16[656,1024]{1,0:T(8,128)(2,1)}), (bf16[256,3072]{1,0:T(8,128)(2,1)}, bf16[256,1024]{1,0:T(8,128)(2,1)}, ...) | async-done | bytes 6127632 | tf_op jit(solution)/shard_map/psum | solution.py:439
  612.4 3.6 convert_element_type.116
  617.1 2.7 convert_element_type.120
  619.8 1.8 convert_element_type.122
  (133 shorter events, 23.5 us)
Async XLA Ops:
  7.2 51.6 %all-gather.9.cloned.1.call-start = ((), (), s32[]{:S(2)}) async-start(), calls=%async_computation.4 | async-start | bytes 7864320 | tf_op jit(solution)/shard_map/all_gather | solution.py:460
  7.9 130.7 %all-gather.11.cloned.1.call-start = ((), (), s32[]{:S(2)}) async-start(), calls=%async_computation.5 | async-start | bytes 2621440 | tf_op jit(solution)/shard_map/all_gather | solution.py:461
  8.7 158.8 %all-gather.13.cloned.1.call-start = ((), (), s32[]{:S(2)}) async-start(), calls=%async_computation.6 | async-start | bytes 13434880 | tf_op jit(solution)/shard_map/all_gather | solution.py:462
  9.4 1.3 copy-start.25
  9.4 1.3 copy-start.26
  9.4 7.3 %copy-start.3 = (bf16[2,64,1024]{2,1,0:T(8,128)(2,1)S(1)}, bf16[2,64,1024]{2,1,0:T(8,128)(2,1)}, u32[]{:S(2)}) copy-start(bf16[2,64,1024]{2,1,0:T(8,128)(2,1)} %param.8) | copy-start | bytes 786436
  9.4 198.0 %all-gather.15.cloned.1.call-start = ((), (), s32[]{:S(2)}) async-start(), calls=%async_computation.7 | async-start | bytes 6717440 | tf_op jit(solution)/shard_map/all_gather | solution.py:463
  10.0 318.7 %all-gather.23.cloned.1.call-start = ((), (), s32[]{:S(2)}) async-start(), calls=%async_computation.11 | async-start | bytes 1310720 | tf_op jit(solution)/shard_map/all_gather | solution.py:427
  10.6 330.7 %all-gather.19.cloned.1.call-start = ((), (), s32[]{:S(2)}) async-start(), calls=%async_computation.9 | async-start | bytes 1310720 | tf_op jit(solution)/shard_map/all_gather | solution.py:427
  76.5 1.9 copy-start.12
  86.1 1.4 copy-start.20
  108.1 1.5 copy-start.6
  118.5 1.0 copy-start.1
  119.4 1.0 copy-start
  137.7 0.8 copy-start.9
  141.1 33.6 %copy-start.13 = (bf16[2,64,1024]{2,1,0:T(8,128)(2,1)}, bf16[2,64,1024]{2,1,0:T(8,128)(2,1)S(1)}, u32[]{:S(2)}) copy-start(bf16[2,64,1024]{2,1,0:T(8,128)(2,1)S(1)} %multiply_convert_fusion.1) | copy-start | bytes 786436
  167.4 39.9 %copy-start.17 = (bf16[2,64,1024]{2,1,0:T(8,128)(2,1)S(1)}, bf16[2,64,1024]{2,1,0:T(8,128)(2,1)}, u32[]{:S(2)}) copy-start(bf16[2,64,1024]{2,1,0:T(8,128)(2,1)} %param.15) | copy-start | bytes 786436
  207.4 7.0 %copy-start.4 = (f32[128,5248]{1,0:T(8,128)S(1)}, f32[128,5248]{1,0:T(8,128)}, u32[]{:S(2)}) copy-start(f32[128,5248]{1,0:T(8,128)} %fusion.64) | copy-start | bytes 8060932
  215.2 9.7 %copy-start.7 = (bf16[128,2624]{1,0:T(8,128)(2,1)}, bf16[128,2624]{1,0:T(8,128)(2,1)S(1)}, u32[]{:S(2)}) copy-start(bf16[128,2624]{1,0:T(8,128)(2,1)S(1)} %get-tuple-element.29) | copy-start | bytes 2015236
  228.4 1.0 copy-start.18
  229.5 3.7 copy-start.16
  261.8 1.2 copy-start.2
  274.3 76.6 %all-gather.17.cloned.1.call-start = ((), (), s32[]{:S(2)}) async-start(), calls=%async_computation.8 | async-start | bytes 3932160 | tf_op jit(solution)/shard_map/all_gather | solution.py:427
  274.4 1.2 copy-start.11
  275.6 5.1 copy-start.21
  301.8 1.8 copy-start.5
  306.8 1.1 copy-start.8
  306.8 85.4 %all-gather.21.cloned.1.call-start = ((), (), s32[]{:S(2)}) async-start(), calls=%async_computation.10 | async-start | bytes 6717440 | tf_op jit(solution)/shard_map/all_gather | solution.py:427
  307.9 5.4 copy-start.23
  309.0 6.9 %copy-start.10 = (bf16[2,16,64,64]{3,1,2,0:T(8,128)(2,1)S(1)}, bf16[2,16,64,64]{3,1,2,0:T(8,128)(2,1)}, u32[]{:S(2)}) copy-start(bf16[2,16,64,64]{3,1,2,0:T(8,128)(2,1)} %copy-done.9) | copy-start | bytes 786436
  309.0 7.2 %copy-start.14 = (bf16[2,64,1024]{2,1,0:T(8,128)(2,1)S(1)}, bf16[2,64,1024]{2,1,0:T(8,128)(2,1)}, u32[]{:S(2)}) copy-start(bf16[2,64,1024]{2,1,0:T(8,128)(2,1)} %copy-done.13) | copy-start | bytes 786436
  309.0 16.3 %all-to-all-start.3 = ((bf16[128,4,656]{0,2,1:T(8,128)(2,1)}), bf16[128,4,656]{0,2,1:T(8,128)(2,1)}, u32[]{:S(2)}, u32[]{:S(2)}) async-start(bf16[128,4,656]{0,2,1:T(8,128)(2,1)} %bitcast.134), calls=%async_computation.3 | async-start | bytes 1343488 | tf_op jit(solution)/shard_map/all_to_all | solution.py:431
  325.3 12.5 %all-to-all-start.1 = ((bf16[128,4,256]{2,0,1:T(8,128)(2,1)}), bf16[128,4,256]{2,0,1:T(8,128)(2,1)S(1)}, u32[]{:S(2)}, u32[]{:S(2)}) async-start(bf16[128,4,256]{2,0,1:T(8,128)(2,1)} %copy.56), calls=%async_computation.1 | async-start | bytes 524288 | tf_op jit(solution)/shard_map/all_to_all | solution.py:431
  337.8 9.4 %all-to-all-start = ((bf16[128,4,256]{2,0,1:T(8,128)(2,1)}), bf16[128,4,256]{2,0,1:T(8,128)(2,1)S(1)}, u32[]{:S(2)}, u32[]{:S(2)}) async-start(bf16[128,4,256]{2,0,1:T(8,128)(2,1)} %copy.55), calls=%async_computation | async-start | bytes 524288 | tf_op jit(solution)/shard_map/all_to_all | solution.py:431
  347.3 9.6 %all-to-all-start.2 = ((bf16[128,4,256]{2,0,1:T(8,128)(2,1)}), bf16[128,4,256]{2,0,1:T(8,128)(2,1)S(1)}, u32[]{:S(2)}, u32[]{:S(2)}) async-start(bf16[128,4,256]{2,0,1:T(8,128)(2,1)} %copy.57), calls=%async_computation.2 | async-start | bytes 524288 | tf_op jit(solution)/shard_map/all_to_all | solution.py:431
  350.9 261.5 %all-reduce.5.cloned.1.call-start = ((), (), s32[]{:S(2)}) async-start(), calls=%async_computation.12 | async-start | bytes 12255232 | tf_op jit(solution)/shard_map/psum | solution.py:439
  399.0 51.3 %copy-start.19 = (bf16[2,64,1024]{2,1,0:T(8,128)(2,1)S(1)}, bf16[2,64,1024]{2,1,0:T(8,128)(2,1)}, u32[]{:S(2)}) copy-start(bf16[2,64,1024]{2,1,0:T(8,128)(2,1)} %param.15) | copy-start | bytes 786436
  612.4 3.6 copy-start.24
  612.4 4.7 copy-start.15
  617.1 2.8 copy-start.22
Sparse Core Ops, SparseCore 0:
  9.6 49.1 all-gather.8
  60.3 22.5 all-gather.10
  84.5 82.9 all-gather.12
  168.9 38.4 all-gather.14
  208.8 16.7 all-gather.22
  274.5 22.8 all-gather.18
  306.9 37.9 all-gather.16
  347.0 45.1 all-gather.20
  398.0 214.3 all-reduce.4

commit v2 on v1

--- a/solution.py
+++ b/solution.py
@@ -180,6 +180,95 @@
         ],
         compiler_params=pltpu.CompilerParams(collective_id=collective_id, has_side_effects=True),
     )(blocks)
+
+
+def gather_kernel(spread, chunks, x_ref, o_ref, send_sem, recv_sem, own_sem):
+    ctx, place = lax.axis_index("ctx"), lax.axis_index("fsdp")
+    across = lax.rem(place + 2, 4)
+    beside = place + 1 - 2 * lax.rem(place, 2)
+    half = lax.rem(ctx, 2)
+    other_ctx = ctx + 1 - 2 * half
+    sibling, partner, neighbour = (ctx, beside), (ctx, across), (other_ctx, place)
+    width = x_ref.shape[-1] // (2 * chunks if spread else chunks)
+    mine = half * chunks if spread else 0
+    theirs = (1 - half) * chunks
+
+    def columns(index):
+        return pl.ds(pl.multiple_of(index * width, 128), width)
+
+    def send(src, dst, sem, device):
+        return pltpu.make_async_remote_copy(
+            src_ref=src,
+            dst_ref=dst,
+            send_sem=send_sem.at[sem],
+            recv_sem=recv_sem.at[sem],
+            device_id=device,
+            device_id_type=MESH_ID,
+        )
+
+    def piece(index):
+        return o_ref.at[across, :, columns(index)]
+
+    barrier = pltpu.get_barrier_semaphore()
+    partners = (sibling, partner, neighbour) if spread else (sibling, partner)
+    for device in partners:
+        pl.semaphore_signal(barrier, inc=1, device_id=device, device_id_type=MESH_ID)
+    pl.semaphore_wait(barrier, len(partners))
+    crossing = [
+        send(
+            x_ref.at[:, columns(mine + c)],
+            o_ref.at[place, :, columns(mine + c)],
+            c,
+            partner,
+        )
+        for c in range(chunks)
+    ]
+    for copy in crossing:
+        copy.start()
+    started = list(crossing)
+    whole = send(x_ref, o_ref.at[place], chunks, sibling)
+    whole.start()
+    own = pltpu.make_async_copy(x_ref, o_ref.at[place], own_sem)
+    own.start()
+    turned = []
+    for c in range(chunks):
+        crossing[c].wait_recv()
+        if spread:
+            turn = send(piece(mine + c), piece(mine + c), chunks + 1 + c, neighbour)
+            turn.start()
+            turned.append(turn)
+        hand = send(piece(mine + c), piece(mine + c), 2 * chunks + 1 + c, sibling)
+        hand.start()
+        started.append(hand)
+    handed = started[chunks:]
+    for c in range(len(turned)):
+        turned[c].wait_recv()
+        hand = send(piece(theirs + c), piece(theirs + c), 3 * chunks + 1 + c, sibling)
+        hand.start()
+        handed.append(hand)
+    whole.wait_recv()
+    own.wait()
+    for hand in handed:
+        hand.wait_recv()
+    for copy in crossing + turned + handed + [whole]:
+        copy.wait_send()
+
+
+def gather(block, spread, chunks, collective_id):
+    rows, width = block.shape
+    count = 4 * chunks + 1
+    return pl.pallas_call(
+        functools.partial(gather_kernel, spread, chunks),
+        out_shape=jax.ShapeDtypeStruct((4, rows, width), block.dtype),
+        in_specs=[pl.BlockSpec(memory_space=pl.ANY)],
+        out_specs=pl.BlockSpec(memory_space=pl.ANY),
+        scratch_shapes=[
+            pltpu.SemaphoreType.DMA((count,)),
+            pltpu.SemaphoreType.DMA((count,)),
+            pltpu.SemaphoreType.DMA,
+        ],
+        compiler_params=pltpu.CompilerParams(collective_id=collective_id, has_side_effects=True),
+    )(block).reshape(4 * rows, width)
 
 
 def pack(blocks):
@@ -316,7 +405,7 @@
     return context_low, (queries, key_rows, value_rows, context, log_total)
 
 
-def by_head_back(context_grad, saved, scaling):
+def by_head_back(context_grad, saved, scaling, after):
     seq_count, row_count, head_count, head_size = context_grad.shape
     ctx_count, fsdp_count = lax.axis_size("ctx"), lax.axis_size("fsdp")
     count = ctx_count * fsdp_count
@@ -338,6 +427,7 @@
         ],
         axis=1,
     )
+    sent, after = lax.optimization_barrier((sent, after))
     got = exchange(sent, ctx_count, fsdp_count, 4)
     parts = jnp.stack(
         [got[:, :row_count, :head_size], got[:, :row_count, head_size:], unpack(got[:, row_count:])]
@@ -346,7 +436,7 @@
         parts.reshape(3, seq_count, head_count, row_count, head_size)
         .transpose(1, 3, 0, 2, 4)
         .reshape(seq_count * row_count, 3 * head_count * head_size)
-    )
+    ), after
 
 
 def by_block_forward(mixed_rows, cos_table, sin_table, scaling):
@@ -379,7 +469,7 @@
     return context_low, (queries, key_block, value_block, context, log_total, cos_table, sin_table)
 
 
-def by_block_back(context_grad, saved, scaling):
+def by_block_back(context_grad, saved, scaling, after):
     seq_count, row_count, head_count, head_size = context_grad.shape
     width = head_count * head_size
     queries, key_block, value_block, context, log_total, cos_table, sin_table = saved
@@ -420,24 +510,33 @@
         jnp.stack([query_pre, key_pre, own(value_grad)], axis=2)
         .reshape(seq_count * row_count, 3 * width)
         .astype(jnp.bfloat16)
-    )
+    ), after
 
 
 def group_rows(rows):
     return lax.all_gather(rows, "fsdp", axis=0, tiled=True)
 
 
-def group_columns(rows):
-    return lax.all_to_all(rows, "fsdp", split_axis=1, concat_axis=0, tiled=True)
+def group_columns(arrays):
+    count = lax.axis_size("fsdp")
+    widths = [rows.shape[1] // count for rows in arrays]
+    sent = jnp.stack(
+        [
+            jnp.concatenate(
+                [rows[:, f * width : (f + 1) * width] for rows, width in zip(arrays, widths)],
+                axis=1,
+            )
+            for f in range(count)
+        ]
+    )
+    got = lax.all_to_all(sent, "fsdp", split_axis=0, concat_axis=0, tiled=True)
+    got = got.reshape(-1, sum(widths))
+    edges = [sum(widths[:i]) for i in range(len(widths) + 1)]
+    return [got[:, edges[i] : edges[i + 1]] for i in range(len(widths))]
 
 
 def weight_grad(left, right):
     return jnp.einsum("tw,tf->wf", left, right, preferred_element_type=jnp.float32)
-
-
-def sum_blocks(grads):
-    low = lax.psum(tuple(grad.astype(jnp.bfloat16) for grad in grads), "ctx")
-    return tuple(grad.astype(jnp.float32) for grad in low)
 
 
 def on_device(inputs, attn_gain, attn_proj, attn_out, mlp_gain, mlp_in, mlp_out, cotangent):
@@ -456,8 +555,12 @@
         jnp.float32
     )
     gain_one, gain_two = gains[0], gains[1]
+    ctx_count = lax.axis_size("ctx")
+    small = one_head_each and fsdp_count == 4 and ctx_count == 8
     proj_full, out_full, lift_full, down_full = (
-        lax.all_gather(attn_proj, "fsdp", axis=0, tiled=True),
+        gather(attn_proj, True, 3, 6)
+        if small
+        else lax.all_gather(attn_proj, "fsdp", axis=0, tiled=True),
         lax.all_gather(attn_out, "fsdp", axis=0, tiled=True),
         lax.all_gather(mlp_in, "fsdp", axis=0, tiled=True),
         lax.all_gather(mlp_out, "fsdp", axis=0, tiled=True),
@@ -501,21 +604,37 @@
         .astype(jnp.bfloat16)
         .reshape(seq_count, row_count, head_count, head_size)
     )
-    lift_grad = weight_grad(group_columns(normed_two_low), group_rows(lifted_grad))
-    down_grad = weight_grad(group_columns(gate_low), group_rows(seed_rows))
-    out_grad = weight_grad(group_columns(context_low), group_rows(middle_low))
-    lift_sum, down_sum, out_sum = sum_blocks((lift_grad, down_grad, out_grad))
-    mixed_grad = attention_back(context_grad, saved, scaling)
+    normed_two_part, gate_part, context_part, normed_part = group_columns(
+        (normed_two_low, gate_low, context_low, normed_low)
+    )
+    seed_group = group_rows(seed_rows)
+    joined = group_rows(jnp.concatenate([lifted_grad, middle_low], axis=1))
+    lift_grad = weight_grad(normed_two_part, joined[:, : lifted_grad.shape[1]])
+    out_grad = weight_grad(context_part, joined[:, lifted_grad.shape[1] :])
+    down_grad = weight_grad(gate_part, seed_group)
+    first_grads = tuple(grad.astype(jnp.bfloat16) for grad in (lift_grad, down_grad, out_grad))
+    mixed_grad, first_grads = attention_back(context_grad, saved, scaling, first_grads)
+    first_sums = lax.psum(first_grads, "ctx")
     normed_grad = jnp.einsum(
         "tm,wm->tw", mixed_grad, proj_full, preferred_element_type=jnp.float32
     ).reshape(seq_count, row_count, model_width)
     state_part, gain_one_grad = norm_back_one(normed_grad)
     input_grad = middle_grad + state_part
-    proj_grad = weight_grad(group_columns(normed_low), group_rows(mixed_grad))
-    (proj_sum,) = sum_blocks((proj_grad,))
-    gain_sums = lax.psum(jnp.stack([gain_one_grad, gain_two_grad]), ("ctx", "fsdp"))
+    mixed_group = gather(mixed_grad, False, 4, 7) if small else group_rows(mixed_grad)
+    proj_grad = weight_grad(normed_part, mixed_group).astype(jnp.bfloat16)
+    proj_grad, first_sums = lax.optimization_barrier((proj_grad, first_sums))
+    proj_sum = lax.psum(proj_grad, "ctx").astype(jnp.float32)
+    lift_sum, down_sum, out_sum = (total.astype(jnp.float32) for total in first_sums)
     gain_width = attn_gain.shape[0]
-    gain_own = lax.dynamic_slice_in_dim(gain_sums, fsdp_place * gain_width, gain_width, axis=1)
+    gain_grads = jnp.stack([gain_one_grad, gain_two_grad])
+    if small:
+        shares = gain_grads.reshape(2, fsdp_count, gain_width).transpose(1, 0, 2)
+        shares = jnp.concatenate([shares, jnp.zeros((fsdp_count, 6, gain_width))], axis=1)
+        shares = jnp.concatenate([shares] * ctx_count, axis=0)
+        gain_own = jnp.sum(exchange(shares, ctx_count, fsdp_count, 5), axis=0)
+    else:
+        gain_sums = lax.psum(gain_grads, ("ctx", "fsdp"))
+        gain_own = lax.dynamic_slice_in_dim(gain_sums, fsdp_place * gain_width, gain_width, axis=1)
     return (
         outputs,
         input_grad,

time: 635 us -> 590 us (0.929)
  Pallas kernels: 87.1 us -> 209 us
  waiting for transfers between devices: 317 us -> 199 us
  blocking collectives: 51.2 us -> 5.97 us
  starting transfers between devices: 15.1 us -> 4.72 us
  local copies, waits for them, and re-layouts: 41.7 us -> 50.2 us
    pallas_call x0 -> x2, Pallas kernels: none -> 77.8 us  [gather(): pl.pallas_call(functools.partial(gather_kernel, spread, chunks), out_shap...]
    psum x1 -> x0, blocking collectives: 45.2 us -> none  [on_device(): lax.psum(jnp.stack([gain_one_grad, gain_two_grad]), ('ctx', 'fsdp'))]
    pallas_call x4 -> x5, Pallas kernels: 64.5 us -> 108 us  [exchange(): pl.pallas_call(functools.partial(exchange_kernel, ctx_count, fsdp_count),...]
    all_gather x1 -> x0, waiting for transfers between devices: 39.3 us -> none  [on_device(): lax.all_gather(attn_proj, 'fsdp', axis=0, tiled=True)]
    all_gather x4 -> x2, waiting for transfers between devices: 35.3 us -> 0.02 us  [group_rows(): return lax.all_gather(rows, 'fsdp', axis=0, tiled=True)]
    all_gather x1, waiting for transfers between devices: 26.4 us -> 0.02 us  [on_device(): lax.all_gather(mlp_in, 'fsdp', axis=0, tiled=True)]
    all_to_all x4 -> x1, waiting for transfers between devices: 18.5 us -> 0.01 us  [group_columns(): got = lax.all_to_all(sent, 'fsdp', split_axis=0, concat_axis=0, tiled=True)]
    psum x1 -> x2, waiting for transfers between devices: 161 us -> 179 us  [the longest x1 108 us: on_device(): first_sums = lax.psum(first_grads, 'ctx')]
  transfers between devices with their start and end apart: 13 -> 8, of which waited for: 9 -> 3; matrix products, arithmetic and copies ran while one was open for 20% -> 22% of each run, Pallas kernels for 14% -> 36%
where the time goes in v2:
time: 590 us; the launch traced here: 584 us
  Pallas kernels  209 us (35%)
  waiting for transfers between devices  199 us (34%)
  matrix products  51.3 us (9%)
  local copies, waits for them, and re-layouts  50.2 us (9%)
  other arithmetic  48.4 us (8%)
  between operations  15.4 us (3%)
  blocking collectives  5.97 us (1%)
    pallas_call x5, Pallas kernels, exchange(): pl.pallas_call(functools.partial(exchange_kernel, ctx_count, fsdp_count),...  108 us
    psum x1, waiting for transfers between devices, on_device(): first_sums = lax.psum(first_grads, 'ctx')  108 us
    pallas_call x2, Pallas kernels, gather(): pl.pallas_call(functools.partial(gather_kernel, spread, chunks), out_shap...  77.8 us
    psum x1, waiting for transfers between devices, on_device(): proj_sum = lax.psum(proj_grad, 'ctx').astype(jnp.float32)  71.1 us
    all_gather x1, waiting for transfers between devices, on_device(): lax.all_gather(mlp_out, 'fsdp', axis=0, tiled=True)  17.5 us
    dot_general x4, matrix products, weight_grad(): jnp.einsum('tw,tf->wf', left, right, preferred_element_type=jnp.float32)  15 us
    pallas_call x1, Pallas kernels, attend_back(): pl.pallas_call(attend_back_kernel, grid=(rows // block,), out_shape=(jax....  14.1 us
  transfers between devices with their start and end apart: 8, of which 3 were waited for; matrix products, arithmetic and copies ran while one was open for 22% of the time, Pallas kernels for 36%

profile of v2, /device:TPU:0, one launch (start us, length us, event | category | flops | bytes accessed | tf_op | source)
XLA Modules:
  0.0 584.1 jit_solution(5781894281519306092)
XLA Ops:
  11.0 6.0 %all_gather.18 = bf16[2,1024]{1,0:T(2,128)(2,1)S(1)} all-gather(bf16[2,256]{1,0:T(2,128)(2,1)S(1)} %pad_maximum_fusion.10), channel_id=1, replica_groups=mesh['ctx'=8,'fsdp'=4] {'fsdp'}, dimensions={1}, use_global_device_ids=true | all-gather | bytes 5120 | tf_op jit(solution)/shard_map/all_gather | solution.py:554
  17.0 51.1 %shard_map.143 = bf16[4,256,3072]{2,1,0:T(8,128)(2,1)} custom-call(bf16[256,3072]{1,0:T(8,128)(2,1)} %x_ref.1), custom_call_target="tpu_custom_call" | custom-call | tf_op jit(solution)/shard_map/pallas_call | solution.py:260
  68.1 8.7 %copy.56 = bf16[1024,3072]{0,1:T(8,128)(2,1)} copy(bf16[1024,3072]{1,0:T(8,128)(2,1)} %bitcast.117) | data formatting | bytes 12582912 | tf_op jit(solution)/shard_map/reshape | solution.py:271
  77.0 4.5 fusion.43
  81.5 1.5 slice_bitcast_fusion.1
  84.0 2.8 slice_negate_fusion.2
  86.7 1.0 fusion.36
  87.8 2.0 copy.58
  89.8 2.2 fusion.34
  92.0 1.4 copy.59
  93.8 1.3 maximum_maximum_fusion.x_ref
  95.1 18.5 %shard_map.144 = bf16[32,96,128]{2,1,0:T(8,128)(2,1)} custom-call(bf16[32,96,128]{2,1,0:T(8,128)(2,1)} %maximum_maximum_fusion.x_ref), custom_call_target="tpu_custom_call" | custom-call | tf_op jit(solution)/shard_map/pallas_call | solution.py:171
  113.6 1.3 fusion.55
  115.3 8.5 %shard_map.145 = (f32[2048,64]{1,0:T(8,128)S(1)}, f32[2048,1]{1,0:T(8,128)S(1)}) custom-call(bf16[2048,64]{1,0:T(8,128)(2,1)S(1)} %bitcast.114, bf16[2048,64]{1,0:T(8,128)(2,1)S(1)} %bitcast.112, bf16[2048,64]{1,0:T(8,128)(2,1)S(1)} %bitcast.110), custom_call_target="tpu_custom_call" | custom-call | tf_op jit(solution)/shard_map/pallas_call | solution.py:304
  125.8 15.6 %shard_map.146 = bf16[32,32,128]{2,1,0:T(8,128)(2,1)} custom-call(bf16[32,32,128]{2,1,0:T(8,128)(2,1)} %pad_maximum_fusion.7.x_ref), custom_call_target="tpu_custom_call" | custom-call | tf_op jit(solution)/shard_map/pallas_call | solution.py:171
  141.5 1.2 fusion.66
  143.9 2.1 fusion.69
  146.5 7.3 %fusion.70 = f32[128,5248]{1,0:T(8,128)} fusion(bf16[128,1024]{1,0:T(8,128)(2,1)S(1)} %bitcast.122, bf16[1024,5248]{1,0:T(8,128)(2,1)} %all-gather.8.cloned.1.call-done), kind=kOutput, calls=%fused_computation.145 | convolution fusion | flops 1375731712 | bytes 13697024 | tf_op jit(solution)/shard_map/dot_general | solution.py:584
  153.8 17.5 %all-gather.10.cloned.1.call-done = bf16[2624,1024]{1,0:T(8,128)(2,1)} async-done(((bf16[656,1024]{1,0:T(8,128)(2,1)}), bf16[2624,1024]{1,0:T(8,128)(2,1)}) %all-gather.10.cloned.1.call-update) | async-done | bytes 5373968 | tf_op jit(solution)/shard_map/all_gather | solution.py:566
  171.2 7.0 %fusion.38 = (f32[128,2624]{1,0:T(8,128)S(1)}, f32[128,2624]{1,0:T(8,128)S(1)}, f32[128,2624]{1,0:T(8,128)S(1)}) fusion(f32[128,5248]{1,0:T(8,128)} %fusion.70, bf16[128,1024]{1,0:T(8,128)(2,1)S(1)} %bitcast.127, bf16[2624,1024]{1,0:T(8,128)(2,1)} %all-gather.10.cloned.1.call-done), kind=kOutput, calls=%fused_computation.89 | convolution fusion | flops 709697536 | bytes 11010048 | tf_op jit(solution)/shard_map/td,fd->tf/dot_general | solution.py:594
  179.4 3.5 copy-done.2
  182.8 3.6 fusion.72
  186.7 3.5 fusion.71
  190.2 1.1 add_add_fusion.1
  191.3 1.3 reduce_sum.105
  192.6 1.2 fusion.39
  194.5 1.3 pad_maximum_fusion
  195.8 1.0 copy-done.14
  199.7 1.2 fusion.57
  200.9 1.1 concatenate.102
  202.1 2.0 concatenate.103
  204.1 2.0 concatenate.104
  206.0 1.8 concatenate.105
  207.9 2.6 pad_maximum_fusion.1
  210.4 2.6 copy.66
  213.0 4.4 all-to-all-start
  217.5 3.1 convolution_convert_fusion.4
  220.6 1.3 reshape.251
  223.0 33.2 %shard_map.147 = bf16[32,32,128]{2,1,0:T(8,128)(2,1)} custom-call(bf16[32,32,128]{2,1,0:T(8,128)(2,1)} %pad_maximum_fusion.8.x_ref), custom_call_target="tpu_custom_call" | custom-call | tf_op jit(solution)/shard_map/pallas_call | solution.py:171
  256.2 1.2 fusion.65
  257.6 14.1 %shard_map.148 = (f32[2048,64]{1,0:T(8,128)S(1)}, f32[2048,64]{1,0:T(8,128)S(1)}, f32[2048,64]{1,0:T(8,128)S(1)}) custom-call(bf16[2048,64]{1,0:T(8,128)(2,1)S(1)} %bitcast.115, bf16[2048,64]{1,0:T(8,128)(2,1)S(1)} %bitcast.113, bf16[2048,64]{1,0:T(8,128)(2,1)S(1)} %bitcast.111, f32[2048,64]{1,0:T(8,128)} %copy-done, f32[2048,1]{1,0:T(8,128)} %copy-done.1, ...), custom_call_target="tpu_custom_call" | custom-call | tf_op jit(solution)/shard_map/pallas_call | solution.py:355
  271.7 3.8 multiply_multiply_fusion.5
  275.9 4.8 fusion.18
  281.0 4.0 fusion.19
  285.1 1.3 maximum_maximum_fusion.1.x_ref
  286.4 1.5 copy_bitcast_fusion
  287.9 3.7 convolution_convert_fusion.2
  291.7 2.5 convolution_convert_fusion.3
  294.1 5.6 convolution_convert_fusion
  299.8 31.1 %shard_map.149 = bf16[32,96,128]{2,1,0:T(8,128)(2,1)} custom-call(bf16[32,96,128]{2,1,0:T(8,128)(2,1)} %maximum_maximum_fusion.1.x_ref), custom_call_target="tpu_custom_call" | custom-call | tf_op jit(solution)/shard_map/pallas_call | solution.py:171
  331.0 1.5 fusion.53
  334.6 1.9 reshape.260.x_ref
  336.4 1.1 dot_general.57
  337.6 26.7 %shard_map.151 = bf16[4,128,3072]{2,1,0:T(8,128)(2,1)} custom-call(bf16[128,3072]{1,0:T(8,128)(2,1)} %reshape.260.x_ref), custom_call_target="tpu_custom_call" | custom-call | tf_op jit(solution)/shard_map/pallas_call | solution.py:260
  364.3 5.3 fusion.33
  370.0 3.1 convolution_convert_fusion.1
  373.1 108.3 %all-reduce.9.cloned.1.call-done = (bf16[256,5248]{1,0:T(8,128)(2,1)}, bf16[656,1024]{1,0:T(8,128)(2,1)}, bf16[256,1024]{1,0:T(8,128)(2,1)}) async-done(((bf16[256,5248]{1,0:T(8,128)(2,1)}, bf16[656,1024]{1,0:T(8,128)(2,1)}, bf16[256,1024]{1,0:T(8,128)(2,1)}), (bf16[256,5248]{1,0:T(8,128)(2,1)}, bf16[656,1024]{1,0:T(8,128)(2,1)}, bf16[256,1024]{1,0:T(8,128)(2,1)})) %all-reduce.9.cloned.1.call-update) | async-done | bytes 4554768 | tf_op jit(solution)/shard_map/psum | solution.py:617
  482.2 9.9 %shard_map.150 = f32[32,8,256]{2,1,0:T(8,128)} custom-call(f32[32,8,256]{2,1,0:T(8,128)} %copy-done.26), custom_call_target="tpu_custom_call" | custom-call | tf_op jit(solution)/shard_map/pallas_call | solution.py:171
  493.7 1.1 add_add_fusion.2
  494.7 4.6 convert_element_type.121
  499.4 1.8 convert_element_type.122
  501.2 1.1 convert_element_type.120
  502.3 71.1 %all-reduce.7.cloned.1.call-done = bf16[256,3072]{1,0:T(8,128)(2,1)} async-done(((bf16[256,3072]{1,0:T(8,128)(2,1)}), bf16[256,3072]{1,0:T(8,128)(2,1)}) %all-reduce.7.cloned.1.call-update) | async-done | bytes 1572880 | tf_op jit(solution)/shard_map/psum | solution.py:626
  573.4 3.4 convert_element_type.119
  (154 shorter events, 21.2 us)
Async XLA Ops:
  7.2 136.8 %all-gather.6.cloned.1.call-start = ((), (), s32[]{:S(2)}) async-start(), calls=%async_computation.1 | async-start | bytes 2621440 | tf_op jit(solution)/shard_map/all_gather | solution.py:564
  7.9 138.6 %all-gather.8.cloned.1.call-start = ((), (), s32[]{:S(2)}) async-start(), calls=%async_computation.2 | async-start | bytes 13434880 | tf_op jit(solution)/shard_map/all_gather | solution.py:565
  8.7 1.4 copy-start.3
  8.7 1.8 copy-start.33
  8.7 1.8 copy-start.34
  8.7 162.5 %all-gather.10.cloned.1.call-start = ((), (), s32[]{:S(2)}) async-start(), calls=%async_computation.3 | async-start | bytes 6717440 | tf_op jit(solution)/shard_map/all_gather | solution.py:566
  9.4 278.5 %all-gather.14.cloned.1.call-start = ((), (), s32[]{:S(2)}) async-start(), calls=%async_computation.5 | async-start | bytes 1310720 | tf_op jit(solution)/shard_map/all_gather | solution.py:517
  10.0 281.7 %all-gather.12.cloned.1.call-start = ((), (), s32[]{:S(2)}) async-start(), calls=%async_computation.4 | async-start | bytes 8028160 | tf_op jit(solution)/shard_map/all_gather | solution.py:517
  10.1 73.7 %copy-start.31 = (f32[32]{0:T(128)}, f32[32]{0:T(128)S(1)}, u32[]{:S(2)}) copy-start(f32[32]{0:T(128)S(1)} %negate_power_fusion) | copy-start | bytes 388
  10.4 0.6 copy-start.29
  77.0 4.5 copy-start.23
  92.0 1.4 copy-start.19
  92.0 1.7 copy-start.20
  113.6 1.3 copy-start.10
  123.8 1.0 copy-start.1
  124.8 1.0 copy-start
  143.1 0.8 copy-start.13
  146.5 24.8 %copy-start.17 = (bf16[2,64,1024]{2,1,0:T(8,128)(2,1)S(1)}, bf16[2,64,1024]{2,1,0:T(8,128)(2,1)}, u32[]{:S(2)}) copy-start(bf16[2,64,1024]{2,1,0:T(8,128)(2,1)} %param.15) | copy-start | bytes 786436
  171.2 7.0 %copy-start.7 = (f32[128,5248]{1,0:T(8,128)S(1)}, f32[128,5248]{1,0:T(8,128)}, u32[]{:S(2)}) copy-start(f32[128,5248]{1,0:T(8,128)} %fusion.70) | copy-start | bytes 8060932
  178.2 4.6 copy-start.2
  179.1 7.6 %copy-start.11 = (bf16[128,2624]{1,0:T(8,128)(2,1)}, bf16[128,2624]{1,0:T(8,128)(2,1)S(1)}, u32[]{:S(2)}) copy-start(bf16[128,2624]{1,0:T(8,128)(2,1)S(1)} %get-tuple-element.44) | copy-start | bytes 2015236
  182.8 3.6 copy-start.5
  191.3 3.2 copy-start.6
  192.6 3.2 copy-start.27
  193.8 0.7 copy-start.15
  195.8 1.0 copy-start.14
  195.8 2.1 copy-start.24
  195.8 2.8 copy-start.32
  197.2 2.5 copy-start.12
  213.0 4.5 copy-start.16
  213.0 73.4 %all-to-all-start = ((bf16[4,128,1424]{1,2,0:T(8,128)(2,1)}), bf16[4,128,1424]{1,2,0:T(8,128)(2,1)}, u32[]{:S(2)}, u32[]{:S(2)}) async-start(bf16[4,128,1424]{1,2,0:T(8,128)(2,1)} %copy.66), calls=%async_computation | async-start | bytes 2916352 | tf_op jit(solution)/shard_map/all_to_all | solution.py:532
  217.4 263.9 %all-reduce.9.cloned.1.call-start = ((), (), s32[]{:S(2)}) async-start(), calls=%async_computation.7 | async-start | bytes 9109504 | tf_op jit(solution)/shard_map/psum | solution.py:617
  287.9 6.3 %copy-start.21 = (bf16[512,1424]{0,1:T(8,128)(2,1)}, bf16[512,1424]{0,1:T(8,128)(2,1)S(1)}, u32[]{:S(2)}) copy-start(bf16[512,1424]{0,1:T(8,128)(2,1)S(1)} %copy_bitcast_fusion) | copy-start | bytes 4374532
  299.8 273.6 %all-reduce.7.cloned.1.call-start = ((), (), s32[]{:S(2)}) async-start(), calls=%async_computation.6 | async-start | bytes 3145728 | tf_op jit(solution)/shard_map/psum | solution.py:626
  332.4 1.1 copy-start.9
  364.3 5.3 copy-start.30
  364.3 5.7 copy-start.4
  373.1 120.6 %copy-start.8 = (f32[2,64,1024]{2,1,0:T(8,128)S(1)}, f32[2,64,1024]{2,1,0:T(8,128)}, u32[]{:S(2)}) copy-start(f32[2,64,1024]{2,1,0:T(8,128)} %get-tuple-element.73) | copy-start | bytes 1572868
  373.1 120.6 %copy-start.18 = (bf16[2,64,1024]{2,1,0:T(8,128)(2,1)S(1)}, bf16[2,64,1024]{2,1,0:T(8,128)(2,1)}, u32[]{:S(2)}) copy-start(bf16[2,64,1024]{2,1,0:T(8,128)(2,1)} %param.15) | copy-start | bytes 786436
  373.1 120.6 %copy-start.28 = (f32[2,64]{1,0:T(2,128)S(1)}, f32[2,64]{1,0:T(2,128)}, u32[]{:S(2)}) copy-start(f32[2,64]{1,0:T(2,128)} %copy-done.27) | copy-start | bytes 1540
  481.5 0.7 copy-start.26
  494.7 4.6 copy-start.22
  499.4 1.9 copy-start.25
Sparse Core Ops, SparseCore 0:
  9.6 36.5 all-gather.5
  47.7 80.1 all-gather.7
  129.5 41.6 all-gather.9
  172.6 17.0 all-gather.13
  196.0 65.9 all-gather.11
  299.9 181.3 all-reduce.8
  485.4 87.9 all-reduce.6

commit v3 on v2

--- a/solution.py
+++ b/solution.py
@@ -271,6 +271,202 @@
     )(block).reshape(4 * rows, width)
 
 
+TILE = 16
+SLICE = 1536
+
+
+def total_kernel(pair, lone, x_ref, o_ref, y_got, z_got, z_sent, e_got, send_sem, recv_sem):
+    ctx, place = lax.axis_index("ctx"), lax.axis_index("fsdp")
+    y = lax.rem(ctx, 2)
+    z = ctx // 2
+    firsts, lasts = 2 * pair, 2 * lone
+    every = firsts + lasts
+
+    def send(src, dst, sem, to_ctx):
+        return pltpu.make_async_remote_copy(
+            src_ref=src,
+            dst_ref=dst,
+            send_sem=send_sem.at[sem],
+            recv_sem=recv_sem.at[sem],
+            device_id=(to_ctx, place),
+            device_id_type=MESH_ID,
+        )
+
+    y_side = ctx + 1 - 2 * y
+
+    def rows(item, side):
+        if item < firsts:
+            return pl.ds(pl.multiple_of((side * firsts + item) * TILE, TILE), TILE)
+        return pl.ds((firsts + item) * TILE, TILE)
+
+    def end_of(item):
+        return item // pair if item < firsts else (item - firsts) // lone
+
+    def turn_of(item):
+        return item % pair if item < firsts else (item - firsts) % lone
+
+    def add(store, store_rows, terms):
+        @pl.loop(0, x_ref.shape[1] // SLICE)
+        def _(i):
+            columns = pl.ds(pl.multiple_of(i * SLICE, SLICE), SLICE)
+            total = terms[0][0][terms[0][1], columns].astype(jnp.float32)
+            for ref, place_rows in terms[1:]:
+                total += ref[place_rows, columns].astype(jnp.float32)
+            store[store_rows, columns] = total.astype(jnp.bfloat16)
+
+    def slot(item):
+        return pl.ds(item * TILE, TILE)
+
+    def pair_copy(item):
+        return send(x_ref.at[rows(item, 1 - y), :], y_got.at[slot(item), :], item, y_side)
+
+    def up_copy(item, to_z):
+        return send(z_sent.at[slot(item), :], z_got.at[slot(item), :], firsts + item, 2 * to_z + y)
+
+    def end_copy(item):
+        return send(
+            z_sent.at[slot(item), :],
+            e_got.at[slot(item - firsts), :],
+            firsts + every + item - firsts,
+            y_side,
+        )
+
+    def down_copy(item, to_z):
+        here = rows(item, y)
+        return send(
+            o_ref.at[here, :], o_ref.at[here, :], firsts + every + lasts + item, 2 * to_z + y
+        )
+
+    def back_copy(item):
+        here = rows(item, y)
+        return send(
+            o_ref.at[here, :], o_ref.at[here, :], firsts + 2 * every + lasts + item, y_side
+        )
+
+    barrier = pltpu.get_barrier_semaphore()
+    pl.semaphore_signal(barrier, inc=1, device_id=(y_side, place), device_id_type=MESH_ID)
+
+    @pl.when(z > 0)
+    def _():
+        pl.semaphore_signal(barrier, inc=1, device_id=(ctx - 2, place), device_id_type=MESH_ID)
+
+    @pl.when(z < 3)
+    def _():
+        pl.semaphore_signal(barrier, inc=1, device_id=(ctx + 2, place), device_id_type=MESH_ID)
+
+    @pl.when((z == 0) | (z == 3))
+    def _():
+        pl.semaphore_wait(barrier, 2)
+
+    @pl.when((z > 0) & (z < 3))
+    def _():
+        pl.semaphore_wait(barrier, 3)
+
+    for turn in range(pair):
+        for end in range(2):
+            pair_copy(end * pair + turn).start()
+
+    def steps(my_z):
+        depth = lambda item: 3 - my_z if end_of(item) == 0 else my_z
+        toward = lambda item: my_z - 1 if end_of(item) == 0 else my_z + 1
+        away = lambda item: my_z + 1 if end_of(item) == 0 else my_z - 1
+        events = []
+        for item in range(every):
+            wait = 1 if item < firsts else 0
+            late = 0 if item < firsts else 1
+            at = 2 * turn_of(item) + depth(item) + wait
+            events.append((at, item, "up"))
+            if depth(item) == 3 and late:
+                events.append((at + 1, item, "meet"))
+            if depth(item) < 3:
+                events.append(
+                    (2 * turn_of(item) + 3 + wait + late + 3 - depth(item), item, "down")
+                )
+        pending = []
+
+        def start(copy):
+            copy.start()
+            pending.append(copy)
+
+        def finish(item):
+            if depth(item) > 0:
+                start(down_copy(item, away(item)))
+            if item < firsts:
+                start(back_copy(item))
+
+        for _, item, kind in sorted(events):
+            if kind == "up":
+                terms = [(x_ref, rows(item, y))]
+                if item < firsts:
+                    pair_copy(item).wait_recv()
+                    terms.append((y_got, slot(item)))
+                if depth(item) > 0:
+                    up_copy(item, away(item)).wait_recv()
+                    terms.append((z_got, slot(item)))
+                if depth(item) == 3 and item < firsts:
+                    add(o_ref, rows(item, y), terms)
+                    finish(item)
+                else:
+                    add(z_sent, slot(item), terms)
+                    if depth(item) == 3:
+                        start(end_copy(item))
+                    else:
+                        start(up_copy(item, toward(item)))
+            elif kind == "meet":
+                end_copy(item).wait_recv()
+                add(
+                    o_ref,
+                    rows(item, y),
+                    [(z_sent, slot(item)), (e_got, slot(item - firsts))],
+                )
+                finish(item)
+            else:
+                down_copy(item, toward(item)).wait_recv()
+                finish(item)
+        for copy in pending:
+            copy.wait_send()
+
+    for my_z in range(4):
+        pl.when(z == my_z)(functools.partial(steps, my_z))
+
+    for item in range(firsts):
+        pair_copy(item).wait_send()
+        send(
+            o_ref.at[rows(item, y), :],
+            o_ref.at[rows(item, 1 - y), :],
+            firsts + 2 * every + lasts + item,
+            y_side,
+        ).wait_recv()
+
+
+def total_over_ctx(grads, collective_id):
+    rows, width = grads.shape
+    chunks = rows // TILE
+    pair, lone = chunks // 8, chunks // 4
+    items = 2 * pair + 2 * lone
+    sems = 4 * pair + 2 * items + 2 * lone
+    low = lambda count: pltpu.VMEM((count * TILE, width), jnp.bfloat16)
+    return pl.pallas_call(
+        functools.partial(total_kernel, pair, lone),
+        out_shape=jax.ShapeDtypeStruct((rows, width), jnp.bfloat16),
+        in_specs=[pl.BlockSpec(memory_space=pltpu.VMEM)],
+        out_specs=pl.BlockSpec(memory_space=pltpu.VMEM),
+        scratch_shapes=[
+            low(2 * pair),
+            low(items),
+            low(items),
+            low(2 * lone),
+            pltpu.SemaphoreType.DMA((sems,)),
+            pltpu.SemaphoreType.DMA((sems,)),
+        ],
+        compiler_params=pltpu.CompilerParams(
+            collective_id=collective_id,
+            has_side_effects=True,
+            vmem_limit_bytes=48 * 1024 * 1024,
+        ),
+    )(grads)
+
+
 def pack(blocks):
     half = blocks.shape[-2] // 2
     return jnp.concatenate([blocks[..., :half, :], blocks[..., half:, :]], axis=-1)
@@ -551,6 +747,7 @@
     start_row = (lax.axis_index("ctx") * fsdp_count + fsdp_place) * row_count
     cos_table, sin_table = angles(start_row + jnp.arange(row_count, dtype=jnp.int32), head_size)
     tokens = seq_count * row_count
+    gain_width = own_rows = attn_gain.shape[0]
     gains = lax.all_gather(jnp.stack([attn_gain, mlp_gain]), "fsdp", axis=1, tiled=True).astype(
         jnp.float32
     )
@@ -614,7 +811,6 @@
     down_grad = weight_grad(gate_part, seed_group)
     first_grads = tuple(grad.astype(jnp.bfloat16) for grad in (lift_grad, down_grad, out_grad))
     mixed_grad, first_grads = attention_back(context_grad, saved, scaling, first_grads)
-    first_sums = lax.psum(first_grads, "ctx")
     normed_grad = jnp.einsum(
         "tm,wm->tw", mixed_grad, proj_full, preferred_element_type=jnp.float32
     ).reshape(seq_count, row_count, model_width)
@@ -622,10 +818,28 @@
     input_grad = middle_grad + state_part
     mixed_group = gather(mixed_grad, False, 4, 7) if small else group_rows(mixed_grad)
     proj_grad = weight_grad(normed_part, mixed_group).astype(jnp.bfloat16)
-    proj_grad, first_sums = lax.optimization_barrier((proj_grad, first_sums))
-    proj_sum = lax.psum(proj_grad, "ctx").astype(jnp.float32)
-    lift_sum, down_sum, out_sum = (total.astype(jnp.float32) for total in first_sums)
-    gain_width = attn_gain.shape[0]
+    grads = (*first_grads, proj_grad)
+    if small:
+        sheet = [grad.reshape(own_rows, -1) for grad in grads]
+        widths = [grad.shape[1] for grad in sheet]
+        spare = -sum(widths) % SLICE
+        sheet = jnp.concatenate(
+            [sheet[0], sheet[2], sheet[3], sheet[1], jnp.zeros((own_rows, spare), jnp.bfloat16)],
+            axis=1,
+        )
+        sums = total_over_ctx(sheet, 8)
+        edges = [0, widths[0], widths[0] + widths[2], widths[0] + widths[2] + widths[3]]
+        lift_sum, out_sum, proj_sum, down_sum = (
+            sums[:, edges[0] : edges[1]],
+            sums[:, edges[1] : edges[2]],
+            sums[:, edges[2] : edges[3]],
+            sums[:, edges[3] : edges[3] + widths[1]].reshape(mlp_out.shape),
+        )
+    else:
+        lift_sum, down_sum, out_sum, proj_sum = lax.psum(grads, "ctx")
+    lift_sum, down_sum, out_sum, proj_sum = (
+        total.astype(jnp.float32) for total in (lift_sum, down_sum, out_sum, proj_sum)
+    )
     gain_grads = jnp.stack([gain_one_grad, gain_two_grad])
     if small:
         shares = gain_grads.reshape(2, fsdp_count, gain_width).transpose(1, 0, 2)

time: 590 us -> 578 us (0.980)
  waiting for transfers between devices: 199 us -> 20.1 us
  Pallas kernels: 209 us -> 353 us
  local copies, waits for them, and re-layouts: 50.2 us -> 70.6 us
    psum x2 -> x0, waiting for transfers between devices: 179 us -> none  [the longest x1 108 us: on_device(): first_sums = lax.psum(first_grads, 'ctx')]
    pallas_call x0 -> x1, Pallas kernels: none -> 159 us  [total_over_ctx(): pl.pallas_call(functools.partial(total_kernel, pair, lone), out_shape=jax...]
    pallas_call x5, Pallas kernels: 108 us -> 94.2 us  [exchange(): pl.pallas_call(functools.partial(exchange_kernel, ctx_count, fsdp_count),...]
    concatenate x0 -> x1, local copies, waits for them, and re-layouts: none -> 11.4 us  [on_device(): jnp.concatenate([sheet[0], sheet[2], sheet[3], sheet[1], jnp.zeros((own_r...]
    convert_element_type x3 -> x4, other arithmetic: 7.54 us -> 13.1 us  [on_device(): total.astype(jnp.float32)]
  transfers between devices with their start and end apart: 8 -> 6, of which waited for: 3 -> 1; matrix products, arithmetic and copies ran while one was open for 22% -> 18% of each run, Pallas kernels for 36% -> 25%
where the time goes in v3:
time: 578 us; the launch traced here: 571 us
  Pallas kernels  353 us (61%)
  local copies, waits for them, and re-layouts  70.6 us (12%)
  matrix products  50.9 us (9%)
  other arithmetic  50.5 us (9%)
  waiting for transfers between devices  20.1 us (3%)
  between operations  15.1 us (3%)
  blocking collectives  5.97 us (1%)
    pallas_call x1, Pallas kernels, total_over_ctx(): pl.pallas_call(functools.partial(total_kernel, pair, lone), out_shape=jax...  159 us
    pallas_call x5, Pallas kernels, exchange(): pl.pallas_call(functools.partial(exchange_kernel, ctx_count, fsdp_count),...  94.2 us
    pallas_call x2, Pallas kernels, gather(): pl.pallas_call(functools.partial(gather_kernel, spread, chunks), out_shap...  77.8 us
    all_gather x1, waiting for transfers between devices, on_device(): lax.all_gather(mlp_out, 'fsdp', axis=0, tiled=True)  17.5 us
    dot_general x4, matrix products, weight_grad(): jnp.einsum('tw,tf->wf', left, right, preferred_element_type=jnp.float32)  14.7 us
    pallas_call x1, Pallas kernels, attend_back(): pl.pallas_call(attend_back_kernel, grid=(rows // block,), out_shape=(jax....  14.1 us
    convert_element_type x4, other arithmetic, on_device(): total.astype(jnp.float32)  13.1 us
  transfers between devices with their start and end apart: 6, of which 1 were waited for; matrix products, arithmetic and copies ran while one was open for 18% of the time, Pallas kernels for 25%

profile of v3, /device:TPU:0, one launch (start us, length us, event | category | flops | bytes accessed | tf_op | source)
XLA Modules:
  0.0 571.0 jit_solution(15463182366156632771)
XLA Ops:
  11.0 6.0 %all_gather.18 = bf16[2,1024]{1,0:T(2,128)(2,1)S(1)} all-gather(bf16[2,256]{1,0:T(2,128)(2,1)S(1)} %pad_maximum_fusion.10), channel_id=1, replica_groups=mesh['ctx'=8,'fsdp'=4] {'fsdp'}, dimensions={1}, use_global_device_ids=true | all-gather | bytes 5120 | tf_op jit(solution)/shard_map/all_gather | solution.py:751
  17.0 51.1 %shard_map.143 = bf16[4,256,3072]{2,1,0:T(8,128)(2,1)} custom-call(bf16[256,3072]{1,0:T(8,128)(2,1)} %x_ref.1), custom_call_target="tpu_custom_call" | custom-call | tf_op jit(solution)/shard_map/pallas_call | solution.py:260
  68.1 8.7 %copy.56 = bf16[1024,3072]{0,1:T(8,128)(2,1)} copy(bf16[1024,3072]{1,0:T(8,128)(2,1)} %bitcast.117) | data formatting | bytes 12582912 | tf_op jit(solution)/shard_map/reshape | solution.py:271
  77.0 4.5 fusion.43
  81.5 1.5 slice_bitcast_fusion.1
  84.0 2.8 slice_negate_fusion.2
  87.8 2.0 copy.58
  89.8 2.2 fusion.34
  92.0 1.4 copy.59
  93.8 1.3 maximum_maximum_fusion.x_ref
  95.1 18.5 %shard_map.144 = bf16[32,96,128]{2,1,0:T(8,128)(2,1)} custom-call(bf16[32,96,128]{2,1,0:T(8,128)(2,1)} %maximum_maximum_fusion.x_ref), custom_call_target="tpu_custom_call" | custom-call | tf_op jit(solution)/shard_map/pallas_call | solution.py:171
  113.6 1.2 fusion.55
  115.3 8.5 %shard_map.145 = (f32[2048,64]{1,0:T(8,128)S(1)}, f32[2048,1]{1,0:T(8,128)S(1)}) custom-call(bf16[2048,64]{1,0:T(8,128)(2,1)S(1)} %bitcast.114, bf16[2048,64]{1,0:T(8,128)(2,1)S(1)} %bitcast.112, bf16[2048,64]{1,0:T(8,128)(2,1)S(1)} %bitcast.110), custom_call_target="tpu_custom_call" | custom-call | tf_op jit(solution)/shard_map/pallas_call | solution.py:500
  125.8 15.6 %shard_map.146 = bf16[32,32,128]{2,1,0:T(8,128)(2,1)} custom-call(bf16[32,32,128]{2,1,0:T(8,128)(2,1)} %pad_maximum_fusion.7.x_ref), custom_call_target="tpu_custom_call" | custom-call | tf_op jit(solution)/shard_map/pallas_call | solution.py:171
  141.5 1.2 fusion.66
  143.9 2.1 fusion.69
  146.5 7.3 %fusion.70 = f32[128,5248]{1,0:T(8,128)} fusion(bf16[128,1024]{1,0:T(8,128)(2,1)S(1)} %bitcast.122, bf16[1024,5248]{1,0:T(8,128)(2,1)} %all-gather.8.cloned.1.call-done), kind=kOutput, calls=%fused_computation.149 | convolution fusion | flops 1375731712 | bytes 13697024 | tf_op jit(solution)/shard_map/dot_general | solution.py:781
  153.8 17.5 %all-gather.10.cloned.1.call-done = bf16[2624,1024]{1,0:T(8,128)(2,1)} async-done(((bf16[656,1024]{1,0:T(8,128)(2,1)}), bf16[2624,1024]{1,0:T(8,128)(2,1)}) %all-gather.10.cloned.1.call-update) | async-done | bytes 5373968 | tf_op jit(solution)/shard_map/all_gather | solution.py:763
  171.2 7.0 %fusion.38 = (f32[128,2624]{1,0:T(8,128)S(1)}, f32[128,2624]{1,0:T(8,128)S(1)}, f32[128,2624]{1,0:T(8,128)S(1)}) fusion(f32[128,5248]{1,0:T(8,128)} %fusion.70, bf16[128,1024]{1,0:T(8,128)(2,1)S(1)} %bitcast.127, bf16[2624,1024]{1,0:T(8,128)(2,1)} %all-gather.10.cloned.1.call-done), kind=kOutput, calls=%fused_computation.93 | convolution fusion | flops 709697536 | bytes 11010048 | tf_op jit(solution)/shard_map/td,fd->tf/dot_general | solution.py:791
  179.4 3.5 copy-done.2
  182.8 3.6 fusion.72
  186.7 3.5 fusion.71
  190.3 1.1 add_add_fusion.1
  191.3 1.3 reduce_sum.105
  192.6 1.2 fusion.39
  194.6 1.3 pad_maximum_fusion
  199.7 1.2 fusion.57
  200.9 1.1 concatenate.105
  202.1 2.0 concatenate.106
  204.0 2.0 concatenate.107
  206.0 1.8 concatenate.108
  207.8 2.6 pad_maximum_fusion.1
  210.4 2.6 copy.66
  213.0 4.5 all-to-all-start
  217.4 3.1 convolution_convert_fusion.4
  220.6 1.3 reshape.257
  222.9 33.2 %shard_map.147 = bf16[32,32,128]{2,1,0:T(8,128)(2,1)} custom-call(bf16[32,32,128]{2,1,0:T(8,128)(2,1)} %pad_maximum_fusion.8.x_ref), custom_call_target="tpu_custom_call" | custom-call | tf_op jit(solution)/shard_map/pallas_call | solution.py:171
  256.2 1.2 fusion.65
  257.5 14.1 %shard_map.148 = (f32[2048,64]{1,0:T(8,128)S(1)}, f32[2048,64]{1,0:T(8,128)S(1)}, f32[2048,64]{1,0:T(8,128)S(1)}) custom-call(bf16[2048,64]{1,0:T(8,128)(2,1)S(1)} %bitcast.115, bf16[2048,64]{1,0:T(8,128)(2,1)S(1)} %bitcast.113, bf16[2048,64]{1,0:T(8,128)(2,1)S(1)} %bitcast.111, f32[2048,64]{1,0:T(8,128)} %copy-done, f32[2048,1]{1,0:T(8,128)} %copy-done.1, ...), custom_call_target="tpu_custom_call" | custom-call | tf_op jit(solution)/shard_map/pallas_call | solution.py:551
  271.7 3.8 multiply_multiply_fusion.5
  275.9 4.8 fusion.18
  281.0 4.0 fusion.19
  285.1 1.3 maximum_maximum_fusion.1.x_ref
  286.4 1.5 copy_bitcast_fusion
  287.9 3.7 convolution_convert_fusion.2
  291.6 2.5 convolution_convert_fusion.3
  294.0 5.6 convolution_convert_fusion
  299.7 18.1 %shard_map.149 = bf16[32,96,128]{2,1,0:T(8,128)(2,1)} custom-call(bf16[32,96,128]{2,1,0:T(8,128)(2,1)} %maximum_maximum_fusion.1.x_ref), custom_call_target="tpu_custom_call" | custom-call | tf_op jit(solution)/shard_map/pallas_call | solution.py:171
  317.8 1.6 fusion.53
  321.2 2.1 reshape.266.x_ref
  323.3 26.7 %shard_map.151 = bf16[4,128,3072]{2,1,0:T(8,128)(2,1)} custom-call(bf16[128,3072]{1,0:T(8,128)(2,1)} %reshape.266.x_ref), custom_call_target="tpu_custom_call" | custom-call | tf_op jit(solution)/shard_map/pallas_call | solution.py:260
  350.0 3.0 convolution_convert_fusion.1
  353.0 4.2 reshape.268
  357.8 11.4 %concatenate.113.x_ref = bf16[256,12288]{1,0:T(8,128)(2,1)} concatenate(bf16[256,5248]{1,0:T(8,128)(2,1)} %convolution_convert_fusion, bf16[256,1024]{1,0:T(8,128)(2,1)} %convolution_convert_fusion.3, bf16[256,3072]{1,0:T(8,128)(2,1)S(1)} %convolution_convert_fusion.1, bf16[256,2624]{1,0:T(8,128)(2,1)} %reshape.268, bf16[256,320]{1,0:T(8,128)(2,1)} %broadcast_in_dim.28), dimensions={1} | concatenate | bytes 12582912 | tf_op jit(solution)/shard_map/concatenate | solution.py:826
  369.2 158.6 %shard_map.152 = bf16[256,12288]{1,0:T(8,128)(2,1)} custom-call(bf16[256,12288]{1,0:T(8,128)(2,1)} %concatenate.113.x_ref), custom_call_target="tpu_custom_call" | custom-call | tf_op jit(solution)/shard_map/pallas_call | solution.py:449
  527.8 3.0 slice_convert_fusion.2
  530.9 4.5 slice_convert_fusion
  535.4 3.4 slice_convert_fusion.1
  538.8 2.1 slice_convert_fusion.4
  540.9 1.1 dot_general.57
  542.0 4.3 reshape.269
  546.3 5.1 fusion.33
  552.6 8.8 %shard_map.150 = f32[32,8,256]{2,1,0:T(8,128)} custom-call(f32[32,8,256]{2,1,0:T(8,128)} %copy-done.23), custom_call_target="tpu_custom_call" | custom-call | tf_op jit(solution)/shard_map/pallas_call | solution.py:171
  563.0 1.1 add_add_fusion.2
  (147 shorter events, 23.4 us)
Async XLA Ops:
  7.2 136.8 %all-gather.6.cloned.1.call-start = ((), (), s32[]{:S(2)}) async-start(), calls=%async_computation.1 | async-start | bytes 2621440 | tf_op jit(solution)/shard_map/all_gather | solution.py:761
  7.9 138.6 %all-gather.8.cloned.1.call-start = ((), (), s32[]{:S(2)}) async-start(), calls=%async_computation.2 | async-start | bytes 13434880 | tf_op jit(solution)/shard_map/all_gather | solution.py:762
  8.7 1.4 copy-start.3
  8.7 1.8 copy-start.30
  8.7 1.8 copy-start.31
  8.7 162.5 %all-gather.10.cloned.1.call-start = ((), (), s32[]{:S(2)}) async-start(), calls=%async_computation.3 | async-start | bytes 6717440 | tf_op jit(solution)/shard_map/all_gather | solution.py:763
  9.4 278.5 %all-gather.14.cloned.1.call-start = ((), (), s32[]{:S(2)}) async-start(), calls=%async_computation.5 | async-start | bytes 1310720 | tf_op jit(solution)/shard_map/all_gather | solution.py:713
  10.0 281.6 %all-gather.12.cloned.1.call-start = ((), (), s32[]{:S(2)}) async-start(), calls=%async_computation.4 | async-start | bytes 8028160 | tf_op jit(solution)/shard_map/all_gather | solution.py:713
  10.1 73.7 %copy-start.28 = (f32[32]{0:T(128)}, f32[32]{0:T(128)S(1)}, u32[]{:S(2)}) copy-start(f32[32]{0:T(128)S(1)} %negate_power_fusion) | copy-start | bytes 388
  10.4 0.6 copy-start.26
  77.0 4.5 copy-start.21
  92.0 1.4 copy-start.18
  92.0 1.7 copy-start.19
  113.6 1.3 copy-start.8
  123.8 1.0 copy-start.1
  124.8 1.0 copy-start
  143.1 0.8 copy-start.12
  146.5 24.8 %copy-start.16 = (bf16[2,64,1024]{2,1,0:T(8,128)(2,1)S(1)}, bf16[2,64,1024]{2,1,0:T(8,128)(2,1)}, u32[]{:S(2)}) copy-start(bf16[2,64,1024]{2,1,0:T(8,128)(2,1)} %param.15) | copy-start | bytes 786436
  171.2 7.0 %copy-start.6 = (f32[128,5248]{1,0:T(8,128)S(1)}, f32[128,5248]{1,0:T(8,128)}, u32[]{:S(2)}) copy-start(f32[128,5248]{1,0:T(8,128)} %fusion.70) | copy-start | bytes 8060932
  178.2 4.6 copy-start.2
  179.1 7.6 %copy-start.10 = (bf16[128,2624]{1,0:T(8,128)(2,1)}, bf16[128,2624]{1,0:T(8,128)(2,1)S(1)}, u32[]{:S(2)}) copy-start(bf16[128,2624]{1,0:T(8,128)(2,1)S(1)} %get-tuple-element.33) | copy-start | bytes 2015236
  182.8 3.6 copy-start.4
  191.3 3.2 copy-start.5
  192.6 3.2 copy-start.24
  193.8 0.7 copy-start.14
  195.8 1.0 copy-start.13
  195.8 2.1 copy-start.22
  195.8 2.8 copy-start.29
  197.2 2.5 copy-start.11
  213.0 4.5 copy-start.15
  213.0 73.4 %all-to-all-start = ((bf16[4,128,1424]{1,2,0:T(8,128)(2,1)}), bf16[4,128,1424]{1,2,0:T(8,128)(2,1)}, u32[]{:S(2)}, u32[]{:S(2)}) async-start(bf16[4,128,1424]{1,2,0:T(8,128)(2,1)} %copy.66), calls=%async_computation | async-start | bytes 2916352 | tf_op jit(solution)/shard_map/all_to_all | solution.py:728
  287.9 6.2 %copy-start.20 = (bf16[512,1424]{0,1:T(8,128)(2,1)}, bf16[512,1424]{0,1:T(8,128)(2,1)S(1)}, u32[]{:S(2)}) copy-start(bf16[512,1424]{0,1:T(8,128)(2,1)S(1)} %copy_bitcast_fusion) | copy-start | bytes 4374532
  317.8 1.7 copy-start.9
  546.3 5.1 copy-start.27
  551.4 11.6 %copy-start.7 = (f32[2,64,1024]{2,1,0:T(8,128)S(1)}, f32[2,64,1024]{2,1,0:T(8,128)}, u32[]{:S(2)}) copy-start(f32[2,64,1024]{2,1,0:T(8,128)} %get-tuple-element.62) | copy-start | bytes 1572868
  551.4 11.5 %copy-start.17 = (bf16[2,64,1024]{2,1,0:T(8,128)(2,1)S(1)}, bf16[2,64,1024]{2,1,0:T(8,128)(2,1)}, u32[]{:S(2)}) copy-start(bf16[2,64,1024]{2,1,0:T(8,128)(2,1)} %param.15) | copy-start | bytes 786436
  551.4 11.5 %copy-start.25 = (f32[2,64]{1,0:T(2,128)S(1)}, f32[2,64]{1,0:T(2,128)}, u32[]{:S(2)}) copy-start(f32[2,64]{1,0:T(2,128)} %copy-done.24) | copy-start | bytes 1540
  551.9 0.7 copy-start.23
Sparse Core Ops, SparseCore 0:
  9.6 36.5 all-gather.5
  47.7 80.1 all-gather.7
  129.5 41.7 all-gather.9
  172.6 17.0 all-gather.13
  196.0 65.9 all-gather.11
